TPU v7x, 512 devices: a whole 4x8x8 slice. The times are simulated.
512 devices in a mesh: row: 16 (over y_lo, x, core), col: 32 (over z, y_hi).
Axes of the slice: x: 4, y: 8 (y_hi: 4, y_lo: 2; y = y_hi * 2 + y_lo), z: 8, core: 2. Of those that a mesh axis runs over, the one named last changes fastest.
Arguments:
- panel_adjoint: float32 [24576, 512], P('row', 'col'), may hold values from -6 to 6
- panel_factor: float32 [24576, 512], P('row', 'col'), may hold values from -0.0390625 to 0.0390625
- diag_inverse: float32 [512, 512], P('row', 'col'), as said below
- head_factor: float32 [512, 8192], P('row', 'col'), may hold values from -0.25 to 0.25
- below_factor: float32 [24576, 8192], P('row', 'col'), may hold values from -0.0390625 to 0.0390625
- diag_adjoint: float32 [512, 512], P('row', 'col'), may hold values from -6 to 6
- head_adjoint: float32 [512, 8192], P('row', 'col'), may hold values from -6 to 6
- below_adjoint: float32 [24576, 8192], P('row', 'col'), may hold values from -6 to 6
Outputs:
- diag_updated: float32 [512, 512], P('row', 'col')
- head_updated: float32 [512, 8192], P('row', 'col')
- below_updated: float32 [24576, 8192], P('row', 'col')
Inputs may be any that keep to these rules, and one draw needn't show every extreme that they name: `diag_inverse`: upper triangular with a positive diagonal.
All inputs are finite; a program needn't handle non-finite values.
Results may differ from a plain program's by a relative error of at most 0.000084.
Values sent between devices are 32-bit elements; how exact they have to be, the bound alone decides.
No kernel may reach another device: no remote copies, remote signals or barrier semaphores. Data moves between devices by JAX's collectives and lax.ppermute only.
A program may use at most 64 MiB of HBM per device.

v0:
```python
import jax
import jax.numpy as jnp
from jax import lax
from jax.sharding import PartitionSpec as P


def mult(left, right):
    return jnp.dot(left, right, preferred_element_type=jnp.float32, precision=lax.Precision.HIGHEST)


def tmult(left, right):
    return lax.dot_general(
        left,
        right,
        (((0,), (0,)), ((), ())),
        preferred_element_type=jnp.float32,
        precision=lax.Precision.HIGHEST,
    )


def on_device(
    panel_adjoint,
    panel_factor,
    diag_inverse,
    head_factor,
    below_factor,
    diag_adjoint,
    head_adjoint,
    below_adjoint,
):
    inverse_part = lax.all_gather(diag_inverse, "row", axis=0, tiled=True)
    inverse_whole = lax.all_gather(inverse_part, "col", axis=1, tiled=True)
    panel_whole = lax.all_gather(panel_adjoint, "col", axis=1, tiled=True)
    solved = mult(panel_whole, inverse_whole)
    head_whole = lax.all_gather(head_factor, "row", axis=0, tiled=True)
    below_updated = below_adjoint - mult(solved, head_whole)
    head_term = lax.psum_scatter(
        tmult(solved, below_factor), "row", scatter_dimension=0, tiled=True
    )
    diag_term = lax.psum_scatter(
        tmult(solved, panel_factor), "row", scatter_dimension=0, tiled=True
    )
    diag_updated = diag_adjoint - diag_term
    head_updated = head_adjoint - head_term
    return (diag_updated, head_updated, below_updated)


def solution(mesh):
    placed = (
        P("row", "col"),
        P("row", "col"),
        P("row", "col"),
        P("row", "col"),
        P("row", "col"),
        P("row", "col"),
        P("row", "col"),
        P("row", "col"),
    )
    return jax.shard_map(
        on_device,
        mesh=mesh,
        in_specs=placed,
        out_specs=(P("row", "col"), P("row", "col"), P("row", "col")),
        check_vma=False,
    )
```

profile of v0, /device:TPU:16, one launch (start us, length us, event | category | flops | bytes accessed | tf_op | source)
XLA Modules:
  0.0 362.6 jit_solution(11307395783484746684)
XLA Ops:
  7.2 0.0 copy-start
  7.2 0.0 all-gather.6.cloned.1.call-start
  7.2 20.4 %all-gather = f32[16,32,16]{1,2,0:T(8,128)S(1)} all-gather(f32[1,32,16]{1,2,0:T(8,128)} %bitcast.12), channel_id=1, replica_groups=mesh['row'=16,'col'=32] {'row'}, dimensions={0}, use_global_device_ids=true | all-gather | bytes 34816 | tf_op jit(solution)/shard_map/all_gather | solution.py:31
  27.7 0.7 reshape.7
  28.4 0.0 all-gather.6.cloned.1.call-update
  28.4 0.0 all-gather.4.cloned.1.call-start
  28.5 0.7 all-gather.4.cloned.1.call-update
  29.2 0.0 copy-start.3
  29.2 0.0 reduce-scatter.7.cloned.1.call-start
  29.2 83.3 %all-gather.6.cloned.1.call-done = f32[512,512]{0,1:T(8,128)} async-done(((f32[512,16]{0,1:T(8,128)}), f32[512,512]{0,1:T(8,128)}) %all-gather.6.cloned.1.call-update) | async-done | bytes 1048592 | tf_op jit(solution)/shard_map/all_gather | solution.py:32
  112.6 93.1 %all-gather.4.cloned.1.call-done = f32[1536,512]{0,1:T(8,128)} async-done(((f32[1536,16]{0,1:T(8,128)}), f32[1536,512]{0,1:T(8,128)}) %all-gather.4.cloned.1.call-update) | async-done | bytes 3145744 | tf_op jit(solution)/shard_map/all_gather | solution.py:33
  205.7 12.5 %fusion = f32[1536,512]{1,0:T(8,128)S(1)} fusion(f32[1536,512]{0,1:T(8,128)} %all-gather.4.cloned.1.call-done, f32[512,512]{0,1:T(8,128)} %all-gather.6.cloned.1.call-done), kind=kOutput, calls=%fused_computation.1 | convolution fusion | flops 4831838208 | bytes 7340032 | tf_op jit(solution)/shard_map/dot_general | solution.py:8
  218.2 0.0 copy-start.1
  218.2 1.6 copy-done.1
  219.8 0.0 copy-done.3
  219.8 6.0 %fusion.1 = f32[512,16]{1,0:T(8,128)} fusion(f32[1536,512]{1,0:T(8,128)S(1)} %fusion, f32[1536,16]{0,1:T(8,128)S(1)} %copy-done.3), kind=kOutput, calls=%fused_computation.2 | convolution fusion | flops 150994944 | bytes 3276800
  225.8 0.0 reduce-scatter.7.cloned.1.call-update
  225.8 0.0 copy-start.2
  225.8 0.0 reduce-scatter.5.cloned.1.call-start
  225.9 0.0 copy-done
  225.9 7.9 %fusion.2 = f32[512,256]{1,0:T(8,128)} fusion(f32[1536,512]{1,0:T(8,128)} %copy-done.1, f32[1536,256]{1,0:T(8,128)S(1)} %copy-done), kind=kOutput, calls=%fused_computation.3 | convolution fusion | flops 2415919104 | bytes 5242880 | tf_op jit(solution)/shard_map/dot_general | solution.py:12
  233.7 0.0 reduce-scatter.5.cloned.1.call-update
  233.8 0.0 copy-done.4
  233.8 18.9 %all_gather.15 = f32[512,256]{1,0:T(8,128)S(1)} all-gather(f32[32,256]{1,0:T(8,128)S(1)} %copy-done.4), channel_id=1, replica_groups=mesh['row'=16,'col'=32] {'row'}, dimensions={0}, use_global_device_ids=true | all-gather | bytes 557056 | tf_op jit(solution)/shard_map/all_gather | solution.py:35
  252.6 0.0 copy-done.2
  252.6 5.7 %convolution_subtract_fusion = f32[1536,256]{1,0:T(8,128)} fusion(f32[1536,256]{1,0:T(8,128)S(1)} %copy-done.2, f32[1536,512]{1,0:T(8,128)} %copy-done.1, f32[512,256]{1,0:T(8,128)S(1)} %all_gather.15), kind=kOutput, calls=%fused_computation | convolution fusion | flops 2416312320 | bytes 6815744 | tf_op jit(solution)/shard_map/dot_general | solution.py:8
  258.3 29.6 %reduce-scatter.7.cloned.1.call-done = f32[32,16]{1,0:T(8,128)} async-done(((f32[512,16]{1,0:T(8,128)}), f32[32,16]{1,0:T(8,128)}) %reduce-scatter.7.cloned.1.call-update) | async-done | bytes 2064
  288.0 0.8 copy.14
  288.8 0.0 copy-done.6
  288.8 0.6 sub.9
  289.4 65.3 %reduce-scatter.5.cloned.1.call-done = f32[32,256]{1,0:T(8,128)} async-done(((f32[512,256]{1,0:T(8,128)}), f32[32,256]{1,0:T(8,128)}) %reduce-scatter.5.cloned.1.call-update) | async-done | bytes 32784 | tf_op jit(solution)/shard_map/reduce_scatter | solution.py:37
  354.7 1.4 sub.10
  (5 shorter events, 0.1 us)
Async XLA Ops:
  7.2 218.7 %copy-start = (f32[1536,256]{1,0:T(8,128)S(1)}, f32[1536,256]{1,0:T(8,128)}, u32[]{:S(2)}) copy-start(f32[1536,256]{1,0:T(8,128)} %param.12) | copy-start | bytes 4718596
  7.2 105.4 %all-gather.6.cloned.1.call-start = ((), (), s32[]{:S(2)}) async-start(), calls=%async_computation.3 | async-start | bytes 1081344 | tf_op jit(solution)/shard_map/all_gather | solution.py:32
  28.4 177.2 %all-gather.4.cloned.1.call-start = ((), (), s32[]{:S(2)}) async-start(), calls=%async_computation.2 | async-start | bytes 3244032 | tf_op jit(solution)/shard_map/all_gather | solution.py:33
  29.2 190.6 %copy-start.3 = (f32[1536,16]{0,1:T(8,128)S(1)}, f32[1536,16]{0,1:T(8,128)}, u32[]{:S(2)}) copy-start(f32[1536,16]{0,1:T(8,128)} %param.9) | copy-start | bytes 294916
  29.2 258.8 %reduce-scatter.7.cloned.1.call-start = ((), (), s32[]{:S(2)}) async-start(), calls=%async_computation.5 | async-start | bytes 278528
  218.2 1.6 copy-start.1
  225.8 8.0 %copy-start.4 = (f32[32,256]{1,0:T(8,128)S(1)}, f32[32,256]{1,0:T(8,128)}, u32[]{:S(2)}) copy-start(f32[32,256]{1,0:T(8,128)} %param.11) | copy-start | bytes 98308
  225.8 26.8 %copy-start.2 = (f32[1536,256]{1,0:T(8,128)S(1)}, f32[1536,256]{1,0:T(8,128)}, u32[]{:S(2)}) copy-start(f32[1536,256]{1,0:T(8,128)} %param.15) | copy-start | bytes 4718596
  225.8 128.9 %reduce-scatter.5.cloned.1.call-start = ((), (), s32[]{:S(2)}) async-start(), calls=%async_computation.4 | async-start | bytes 557056 | tf_op jit(solution)/shard_map/reduce_scatter | solution.py:37
  252.6 36.1 %copy-start.6 = (f32[32,16]{0,1:T(8,128)S(1)}, f32[32,16]{0,1:T(8,128)}, u32[]{:S(2)}) copy-start(f32[32,16]{0,1:T(8,128)} %param.13) | copy-start | bytes 6148
  252.6 102.0 %copy-start.5 = (f32[32,256]{1,0:T(8,128)S(1)}, f32[32,256]{1,0:T(8,128)}, u32[]{:S(2)}) copy-start(f32[32,256]{1,0:T(8,128)} %param.14) | copy-start | bytes 98308
Sparse Core Ops, SparseCore 0:
  28.6 83.9 all-gather.5
  115.8 89.8 all-gather.3
  225.9 62.0 reduce-scatter.6
  290.9 63.7 reduce-scatter.4
where the time goes:
time: 363 us
  waiting for transfers between devices  272 us (75%)
  blocking collectives  39.3 us (11%)
  matrix products  32 us (9%)
  between operations  13.8 us (4%)
    all_gather x1, waiting for transfers between devices, on_device(): panel_whole = lax.all_gather(panel_adjoint, 'col', axis=1, tiled=True)  93.1 us
    all_gather x1, waiting for transfers between devices, on_device(): inverse_whole = lax.all_gather(inverse_part, 'col', axis=1, tiled=True)  83.3 us
    reduce_scatter x1, waiting for transfers between devices, on_device(): lax.psum_scatter(tmult(solved, below_factor), 'row', scatter_dimension=0,...  65.3 us
    unnamed x5, waiting for transfers between devices  30.4 us
    all_gather x1, blocking collectives, on_device(): inverse_part = lax.all_gather(diag_inverse, 'row', axis=0, tiled=True)  20.4 us
    all_gather x1, blocking collectives, on_device(): head_whole = lax.all_gather(head_factor, 'row', axis=0, tiled=True)  18.9 us
    dot_general x2, matrix products, mult(): jnp.dot(left, right, preferred_element_type=jnp.float32, precision=lax.Pr...  18.2 us
    dot_general x1, matrix products, tmult(): lax.dot_general(left, right, (((0,), (0,)), ((), ())), preferred_element_...  7.85 us
  transfers between devices with their start and end apart: 4, of which 4 were waited for; matrix products, arithmetic and copies ran while one was open for 4% of the time, Pallas kernels for 0%

commit v1 on v0

v1 whole, which is shorter than its diff:
```python
import jax
import jax.numpy as jnp
from jax import lax
from jax.sharding import PartitionSpec as P

ZS = 8
YS = 4


def col_groups():
    near = [[z * YS + h for h in range(YS)] for z in range(ZS)]
    far = [[z * YS + h for z in range(ZS)] for h in range(YS)]
    return near, far


def dot(left, right, dims):
    return lax.dot_general(
        left,
        right,
        (dims, ((), ())),
        preferred_element_type=jnp.float32,
        precision=lax.Precision.HIGH,
    )


def spread(block, axis, groups, size):
    copies = jnp.broadcast_to(block[None], (size,) + block.shape)
    got = lax.all_to_all(copies, axis, 0, 0, tiled=True, axis_index_groups=groups)
    return got.reshape((size * block.shape[0],) + block.shape[1:])


def on_device(
    panel_adjoint,
    panel_factor,
    diag_inverse,
    head_factor,
    below_factor,
    diag_adjoint,
    head_adjoint,
    below_adjoint,
):
    near, far = col_groups()
    rows = head_factor.shape[0]
    width = head_factor.shape[1]
    part = spread(panel_adjoint.T, "col", near, YS)
    part, inverse = lax.optimization_barrier((part, diag_inverse.T))
    panel = lax.all_gather(part, "col", axis=0, tiled=True, axis_index_groups=far)
    inverse = spread(spread(inverse, "col", near, YS), "col", far, ZS)
    packed = spread(jnp.concatenate([head_factor, inverse.T], 1), "row", None, 16)
    head_whole, inverse = packed[:, :width], packed[:, width:]
    weight = dot(inverse, head_whole, ((1,), (0,)))
    factors = jnp.concatenate([below_factor, panel_factor], 1)
    panel, weight, factors = lax.optimization_barrier((panel, weight, factors))
    term = dot(panel, factors, ((1,), (0,)))
    term = dot(inverse, term, ((0,), (0,)))
    parts = lax.all_to_all(term.reshape(16, rows, -1), "row", 0, 0, tiled=True)
    below_updated = below_adjoint - dot(panel, weight, ((0,), (0,)))
    total = parts.sum(0)
    head_updated = head_adjoint - total[:, :width]
    diag_updated = diag_adjoint - total[:, width:]
    return (diag_updated, head_updated, below_updated)


def solution(mesh):
    placed = (P("row", "col"),) * 8
    return jax.shard_map(
        on_device,
        mesh=mesh,
        in_specs=placed,
        out_specs=(P("row", "col"),) * 3,
        check_vma=False,
    )
```

time: 363 us -> 129 us (0.36)
  the two profiles are of different devices: /device:TPU:16 before, /device:TPU:1 now
where the time goes in v1:
time: 129 us
  blocking collectives  48 us (37%)
  waiting for transfers between devices  26.2 us (20%)
  matrix products  16 us (12%)
  between operations  14.1 us (11%)
  starting transfers between devices  13 us (10%)
  other arithmetic  6.32 us (5%)
  local copies, waits for them, and re-layouts  5.1 us (4%)
    all_to_all x3, blocking collectives, spread(): lax.all_to_all(copies, axis, 0, 0, tiled=True, axis_index_groups=groups)  48 us
    all_to_all x1, waiting for transfers between devices, spread(): lax.all_to_all(copies, axis, 0, 0, tiled=True, axis_index_groups=groups)  18.5 us
    dot_general x4, matrix products, dot(): lax.dot_general(left, right, (dims, ((), ())), preferred_element_type=jnp...  16 us
    all_to_all x1, starting transfers between devices, spread(): lax.all_to_all(copies, axis, 0, 0, tiled=True, axis_index_groups=groups)  8.11 us
    all_to_all x1, waiting for transfers between devices, on_device(): parts = lax.all_to_all(term.reshape(16, rows, -1), 'row', 0, 0, tiled=True)  7.72 us
    all_to_all x1, starting transfers between devices, on_device(): parts = lax.all_to_all(term.reshape(16, rows, -1), 'row', 0, 0, tiled=True)  4.88 us
    concatenate x1, other arithmetic, on_device(): factors = jnp.concatenate([below_factor, panel_factor], 1)  3.03 us
    broadcast_in_dim x4, local copies, waits for them, and re-layouts, spread(): copies = jnp.broadcast_to(block[None], (size,) + block.shape)  2.99 us
  transfers between devices with their start and end apart: 3, of which 2 were waited for; matrix products, arithmetic and copies ran while one was open for 11% of the time, Pallas kernels for 0%

profile of v1, /device:TPU:1, one launch (start us, length us, event | category | flops | bytes accessed | tf_op | source)
XLA Modules:
  0.0 128.8 jit_solution(1401097875945356850)
XLA Ops:
  7.2 0.0 all-gather.2.cloned.1.call-start
  7.2 0.9 broadcast_in_dim.10
  8.1 19.0 %all_to_all.25 = f32[4,16,1536]{2,1,0:T(8,128)} all-to-all(f32[4,16,1536]{2,1,0:T(8,128)S(1)} %broadcast_in_dim.10), channel_id=1, replica_groups={{0,1,2,3},{4,5,6,7},{8,9,10,11},{12,13,14,15},{16,17,18,19},{20,21,22,2..., dimensions={0} | all-to-all | bytes 786432 | tf_op jit(solution)/shard_map/all_to_all | solution.py:28
  27.2 0.0 all-gather.2.cloned.1.call-update
  27.2 0.7 broadcast_in_dim.11
  27.9 0.1 reshape.26
  28.0 11.2 %all_to_all.26 = f32[4,1,512]{2,1,0:T(1,128)S(1)} all-to-all(f32[4,1,512]{2,1,0:T(1,128)S(1)} %reshape.26), channel_id=1, replica_groups={{0,1,2,3},{4,5,6,7},{8,9,10,11},{12,13,14,15},{16,17,18,19},{20,21,22,2..., dimensions={0} | all-to-all | bytes 16384 | tf_op jit(solution)/shard_map/all_to_all | solution.py:28
  39.1 0.5 broadcast.3
  39.7 0.7 reduce
  40.3 0.1 reshape.27
  40.4 0.1 copy.27
  40.5 0.1 reshape.28
  40.6 17.8 %all_to_all.27 = f32[8,1,2048]{2,1,0:T(1,128)S(1)} all-to-all(f32[8,1,2048]{2,1,0:T(1,128)S(1)} %reshape.28), channel_id=1, replica_groups={{0,4,8,12,16,20,24,28},{1,5,9,13,17,21,25,29},{2,6,10,14,18,22,26,30},{..., dimensions={0} | all-to-all | bytes 131072 | tf_op jit(solution)/shard_map/all_to_all | solution.py:28
  58.5 0.8 reduce.1
  59.3 0.1 reshape.29
  59.4 0.1 copy.28
  59.5 0.1 reshape.23
  59.6 1.3 %broadcast_in_dim.14 = f32[16,32,768]{2,1,0:T(8,128)} broadcast(f32[32,768]{1,0:T(8,128)S(1)} %pad_maximum_fusion.1), dimensions={1,2} | broadcast | bytes 1671168 | tf_op jit(solution)/shard_map/broadcast_in_dim | solution.py:27
  60.9 8.1 %all-to-all-start.3 = ((f32[16,32,768]{2,1,0:T(8,128)}), f32[16,32,768]{2,1,0:T(8,128)S(1)}, u32[]{:S(2)}, u32[]{:S(2)}) async-start(f32[16,32,768]{2,1,0:T(8,128)} %broadcast_in_dim.14), calls=%async_computation.3 | async-start | bytes 3145728 | tf_op jit(solution)/shard_map/all_to_all | solution.py:28
  69.0 0.3 copy.29
  69.3 3.0 %pad_maximum_fusion = f32[1536,272]{1,0:T(8,128)} fusion(f32[1536,16]{1,0:T(8,128)S(1)} %copy.29, f32[1536,256]{1,0:T(8,128)} %param.12), kind=kLoop, calls=%fused_computation.1 | loop fusion | flops 417792 | bytes 3342336 | tf_op jit(solution)/shard_map/concatenate | solution.py:52
  72.3 18.5 %all-to-all-done.3 = f32[16,32,768]{2,1,0:T(8,128)S(1)} async-done(((f32[16,32,768]{2,1,0:T(8,128)}), f32[16,32,768]{2,1,0:T(8,128)S(1)}, u32[]{:S(2)}, u32[]{:S(2)}) %all-to-all-start.3) | async-done | bytes 1572896 | tf_op jit(solution)/shard_map/all_to_all | solution.py:28
  90.8 1.4 %fusion.2 = f32[512,256]{1,0:T(8,128)} fusion(f32[512,768]{1,0:T(8,128)S(1)} %bitcast.17), kind=kOutput, calls=%fused_computation.4 | convolution fusion | flops 402653184 | bytes 2097152 | tf_op jit(solution)/shard_map/dot_general | solution.py:17
  92.2 5.1 %fusion.5 = f32[512,272]{0,1:T(8,128)S(1)} fusion(f32[512,1536]{1,0:T(8,128)} %all-gather.2.cloned.1.call-done, f32[1536,272]{1,0:T(8,128)} %pad_maximum_fusion), kind=kOutput, calls=%fused_computation.11 | convolution fusion | flops 1283457024 | bytes 5373952 | tf_op jit(solution)/shard_map/dot_general | solution.py:17
  97.3 4.1 %fusion = f32[512,272]{1,0:T(8,128)} fusion(f32[512,272]{0,1:T(8,128)S(1)} %fusion.5, f32[512,768]{1,0:T(8,128)} %bitcast.18), kind=kOutput, calls=%fused_computation.2 | convolution fusion | flops 427819008 | bytes 2162688 | tf_op jit(solution)/shard_map/dot_general | solution.py:17
  101.4 4.9 %all-to-all-start.4 = ((f32[16,32,272]{2,1,0:T(8,128)}), f32[16,32,272]{2,1,0:T(8,128)}, u32[]{:S(2)}, u32[]{:S(2)}) async-start(f32[16,32,272]{2,1,0:T(8,128)} %bitcast.19), calls=%async_computation.4 | async-start | bytes 1572864 | tf_op jit(solution)/shard_map/all_to_all | solution.py:56
  106.3 0.1 copy.31
  106.4 5.4 %convolution_subtract_fusion = f32[1536,256]{1,0:T(8,128)} fusion(f32[1536,256]{1,0:T(8,128)} %param.15, f32[512,1536]{1,0:T(8,128)S(1)} %copy-done, f32[512,256]{1,0:T(8,128)} %fusion.2), kind=kOutput, calls=%fused_computation | convolution fusion | flops 1208352768 | bytes 6815744 | tf_op jit(solution)/shard_map/dot_general | solution.py:17
  111.8 7.7 %all-to-all-done.4 = f32[16,32,272]{2,1,0:T(8,128)} async-done(((f32[16,32,272]{2,1,0:T(8,128)}), f32[16,32,272]{2,1,0:T(8,128)}, u32[]{:S(2)}, u32[]{:S(2)}) %all-to-all-start.4) | async-done | bytes 557088 | tf_op jit(solution)/shard_map/all_to_all | solution.py:56
  119.5 1.2 reduce_sum.9
  120.7 0.6 slice_subtract_fusion
  121.3 0.7 copy.32
  (16 shorter events, 0.1 us)
Async XLA Ops:
  7.2 52.4 %copy-start.4 = (f32[32,256]{1,0:T(8,128)S(1)}, f32[32,256]{1,0:T(8,128)}, u32[]{:S(2)}) copy-start(f32[32,256]{1,0:T(8,128)} %param.11) | copy-start | bytes 98308
  7.2 85.0 %all-gather.2.cloned.1.call-start = ((), (), s32[]{:S(2)}) async-start(), calls=%async_computation.5 | async-start | bytes 3538944 | tf_op jit(solution)/shard_map/all_gather | solution.py:47
  59.6 9.4 %copy-start.2 = (f32[1536,16]{0,1:T(8,128)S(1)}, f32[1536,16]{0,1:T(8,128)}, u32[]{:S(2)}) copy-start(f32[1536,16]{0,1:T(8,128)} %param.9) | copy-start | bytes 294916
  60.9 29.9 %all-to-all-start.3 = ((f32[16,32,768]{2,1,0:T(8,128)}), f32[16,32,768]{2,1,0:T(8,128)S(1)}, u32[]{:S(2)}, u32[]{:S(2)}) async-start(f32[16,32,768]{2,1,0:T(8,128)} %broadcast_in_dim.14), calls=%async_computation.3 | async-start | bytes 3145728 | tf_op jit(solution)/shard_map/all_to_all | solution.py:28
  90.8 1.4 %copy-start.1 = (f32[16,32,768]{2,1,0:T(8,128)}, f32[16,32,768]{2,1,0:T(8,128)S(1)}, u32[]{:S(2)}) copy-start(f32[16,32,768]{2,1,0:T(8,128)S(1)} %all-to-all-done.3) | copy-start | bytes 4718596
  97.3 9.0 %copy-start.5 = (f32[32,16]{0,1:T(8,128)S(1)}, f32[32,16]{0,1:T(8,128)}, u32[]{:S(2)}) copy-start(f32[32,16]{0,1:T(8,128)} %param.13) | copy-start | bytes 6148
  97.3 9.1 %copy-start = (f32[512,1536]{1,0:T(8,128)S(1)}, f32[512,1536]{1,0:T(8,128)}, u32[]{:S(2)}) copy-start(f32[512,1536]{1,0:T(8,128)} %all-gather.2.cloned.1.call-done) | copy-start | bytes 9437188
  101.4 18.1 %all-to-all-start.4 = ((f32[16,32,272]{2,1,0:T(8,128)}), f32[16,32,272]{2,1,0:T(8,128)}, u32[]{:S(2)}, u32[]{:S(2)}) async-start(f32[16,32,272]{2,1,0:T(8,128)} %bitcast.19), calls=%async_computation.4 | async-start | bytes 1572864 | tf_op jit(solution)/shard_map/all_to_all | solution.py:56
  106.4 14.3 %copy-start.3 = (f32[32,256]{1,0:T(8,128)S(1)}, f32[32,256]{1,0:T(8,128)}, u32[]{:S(2)}) copy-start(f32[32,256]{1,0:T(8,128)} %param.14) | copy-start | bytes 98308
Sparse Core Ops, SparseCore 0:
  27.3 52.7 all-gather.1

commit v2 on v1

v2 whole, which is shorter than its diff:
```python
import functools

import jax
import jax.numpy as jnp
from jax import lax
from jax.experimental import pallas as pl
from jax.experimental.pallas import tpu as pltpu
from jax.sharding import PartitionSpec as P

ZS = 8
YS = 4
RS = 16
TILE = 256
FLOPS = 20 * 10**10
VMEM = 14 * 2**20


def col_groups():
    near = [[z * YS + h for h in range(YS)] for z in range(ZS)]
    far = [[z * YS + h for z in range(ZS)] for h in range(YS)]
    return near, far


def z_shift(step):
    return [(z * YS + h, ((z + step) % ZS) * YS + h) for z in range(ZS) for h in range(YS)]


def spread(block, axis, groups, size):
    copies = jnp.broadcast_to(block[None], (size,) + block.shape)
    return lax.all_to_all(copies, axis, 0, 0, tiled=True, axis_index_groups=groups)


def split(x):
    high = x.astype(jnp.bfloat16)
    return high, (x - high.astype(jnp.float32)).astype(jnp.bfloat16)


def dot3(left, right, dims):
    def one(a, b):
        return lax.dot_general(a, b, (dims, ((), ())), preferred_element_type=jnp.float32)

    return one(left[0], right[0]) + (one(left[0], right[1]) + one(left[1], right[0]))


def joined(refs):
    return jnp.concatenate([r[...] for r in refs], 0) if len(refs) > 1 else refs[0][...]


def products(pieces, b_ref, f_ref):
    piece = split(pieces)
    return dot3(piece, split(b_ref[...]), ((1,), (0,))), dot3(piece, split(f_ref[...]), ((1,), (1,)))


def term_kernel(count, *refs):
    b_ref, f_ref, t_ref, s_ref = refs[count:]
    t_ref[...], s_ref[...] = products(joined(refs[:count]), b_ref, f_ref)


def params(**more):
    return pltpu.CompilerParams(vmem_limit_bytes=VMEM, **more)


def terms(pieces, b, f):
    rows = sum(p.shape[0] for p in pieces)
    return pl.pallas_call(
        functools.partial(term_kernel, len(pieces)),
        out_shape=(
            jax.ShapeDtypeStruct((rows, b.shape[1]), jnp.float32),
            jax.ShapeDtypeStruct((rows, f.shape[0]), jnp.float32),
        ),
        compiler_params=params(),
        cost_estimate=pl.CostEstimate(flops=FLOPS, bytes_accessed=0, transcendentals=0),
        name="terms",
    )(*pieces, b, f)


def weight_kernel(width, packed_ref, w_ref, high_ref, low_ref):
    inverse = packed_ref[:, width:]
    w_ref[...] = dot3(split(inverse), split(packed_ref[:, :width]), ((1,), (0,)))
    high_ref[...], low_ref[...] = split(inverse.T)


def weights(packed, width):
    nb = packed.shape[0]
    return pl.pallas_call(
        functools.partial(weight_kernel, width),
        out_shape=(
            jax.ShapeDtypeStruct((nb, width), jnp.float32),
            jax.ShapeDtypeStruct((nb, nb), jnp.bfloat16),
            jax.ShapeDtypeStruct((nb, nb), jnp.bfloat16),
        ),
        compiler_params=params(),
        cost_estimate=pl.CostEstimate(flops=10**9, bytes_accessed=0, transcendentals=0),
        name="weights",
    )(packed)


def head_kernel(group, z_ref, *refs):
    up_ref, down_ref, b_ref, f_ref, high_ref, low_ref = refs[:6]
    found = refs[6:14]
    out_ref, t_scr, s_scr = refs[14:]
    z = z_ref[0]

    def place(offset):
        return pl.ds(pl.multiple_of(lax.rem(z + offset + ZS, ZS) * group, group), group)

    for step in range(ZS // 2):
        t_ref, s_ref = found[2 * step], found[2 * step + 1]
        for part, offset in enumerate((0,) if step == 0 else (-step, step)):
            t_scr[place(offset), :] = t_ref[part * group : (part + 1) * group, :]
            s_scr[place(offset), :] = s_ref[part * group : (part + 1) * group, :]
    last = place(ZS // 2)
    t_scr[last, :], s_scr[last, :] = products(joined((up_ref, down_ref)), b_ref, f_ref)
    turned = (high_ref[...], low_ref[...])
    head = dot3(turned, split(t_scr[...]), ((1,), (0,)))
    diag = dot3(turned, split(s_scr[...]), ((1,), (0,)))
    rows = head.shape[0] // RS
    small = diag.shape[1]
    for r in range(RS):
        out_ref[r, :rows, :] = head[r * rows : (r + 1) * rows]
        for q in range(rows // 8):
            out_ref[r, rows:, q * 64 : q * 64 + small] = diag[r * rows + q * 8 : r * rows + q * 8 + 8]


def head_terms(z, up, down, b, f, turned, found):
    nb = turned[0].shape[0]
    width, small = b.shape[1], f.shape[0]
    args = (up, down, b, f) + turned + found
    return pl.pallas_call(
        functools.partial(head_kernel, nb // ZS),
        out_shape=jax.ShapeDtypeStruct((RS, nb // RS + 8, width), jnp.float32),
        in_specs=[pl.BlockSpec(memory_space=pltpu.SMEM)]
        + [pl.BlockSpec(memory_space=pltpu.VMEM)] * len(args),
        out_specs=pl.BlockSpec(memory_space=pltpu.VMEM),
        scratch_shapes=[pltpu.VMEM((nb, width), jnp.float32), pltpu.VMEM((nb, small), jnp.float32)],
        compiler_params=params(),
        cost_estimate=pl.CostEstimate(flops=10**9, bytes_accessed=0, transcendentals=0),
        name="head_terms",
    )(z, *args)


def below_kernel(group, z_ref, *refs):
    pieces, (w_ref, old_ref, new_ref) = refs[:9], refs[9:]
    z = z_ref[0]
    order = (0, -1, 1, -2, 2, -3, 3, 4)
    weight = jnp.concatenate(
        [
            w_ref[pl.ds(pl.multiple_of(lax.rem(z + k + ZS, ZS) * group, group), group), :]
            for k in order
        ],
        0,
    )
    panel = joined(pieces)
    new_ref[...] = old_ref[...] - dot3(split(panel), split(weight), ((0,), (0,)))


def below_update(z, pieces, weight, old):
    length, width = old.shape
    nb = weight.shape[0]
    return pl.pallas_call(
        functools.partial(below_kernel, nb // ZS),
        grid=(length // TILE,),
        out_shape=jax.ShapeDtypeStruct(old.shape, jnp.float32),
        in_specs=[pl.BlockSpec(memory_space=pltpu.SMEM)]
        + [pl.BlockSpec((p.shape[0], TILE), lambda i: (0, i)) for p in pieces]
        + [
            pl.BlockSpec((nb, width), lambda i: (0, 0)),
            pl.BlockSpec((TILE, width), lambda i: (i, 0)),
        ],
        out_specs=pl.BlockSpec((TILE, width), lambda i: (i, 0)),
        compiler_params=params(),
        cost_estimate=pl.CostEstimate(flops=6 * length * nb * width, bytes_accessed=0, transcendentals=0),
        name="below_update",
    )(z, *pieces, weight, old)


def finish_kernel(parts_ref, head_ref, diag_ref, new_head_ref, new_diag_ref):
    rows = head_ref.shape[0]
    small = diag_ref.shape[0]
    total = parts_ref[0]
    for r in range(1, RS):
        total = total + parts_ref[r]
    new_head_ref[...] = head_ref[...] - total[:rows]
    tail = total[rows:]
    diag = jnp.concatenate([tail[:, q * 64 : q * 64 + small] for q in range(rows // 8)], 0)
    new_diag_ref[...] = diag_ref[...] - diag.T


def finish(parts, head, diag):
    return pl.pallas_call(
        finish_kernel,
        out_shape=(
            jax.ShapeDtypeStruct(head.shape, jnp.float32),
            jax.ShapeDtypeStruct(diag.shape, jnp.float32),
        ),
        compiler_params=params(),
        name="finish",
    )(parts, head, diag)


def on_device(
    panel_adjoint,
    panel_factor,
    diag_inverse,
    head_factor,
    below_factor,
    diag_adjoint,
    head_adjoint,
    below_adjoint,
):
    near, far = col_groups()
    z = (lax.axis_index("col") // YS).astype(jnp.int32).reshape(1)
    rows, width = head_factor.shape
    length, cols = panel_adjoint.shape
    nb = cols * ZS * YS
    group = cols * YS
    factor = panel_factor.T
    corner = jnp.pad(diag_inverse.T, ((0, 0), (0, 128 - rows)))
    part = spread(jnp.concatenate([panel_adjoint.T, corner], 1), "col", near, YS)
    part = part.reshape(group, length + 128)
    up = down = part[:, :length]
    pieces = [up]
    found = terms((up,), below_factor, factor)
    for step in range(1, ZS // 2):
        up = lax.ppermute(up, "col", z_shift(1))
        down = lax.ppermute(down, "col", z_shift(-1))
        found += tuple(terms((up, down), below_factor, factor))
        pieces += [up, down]
    up = lax.ppermute(up[: group // 2], "col", z_shift(1))
    down = lax.ppermute(down[group // 2 :], "col", z_shift(-1))
    pieces += [up, down]
    inverse = spread(part[:, length:], "col", far, ZS).reshape(nb, 128)[:, :rows]
    packed = spread(jnp.concatenate([head_factor, inverse.T], 1), "row", None, RS)
    weight, high, low = weights(packed.reshape(nb, width + nb), width)
    local = head_terms(z, up, down, below_factor, factor, (high, low), tuple(found))
    parts = lax.all_to_all(local, "row", 0, 0, tiled=True)
    below_updated = below_update(z, pieces, weight, below_adjoint)
    head_updated, diag_updated = finish(parts, head_adjoint, diag_adjoint.T)
    return (diag_updated.T, head_updated, below_updated)


def solution(mesh):
    placed = (P("row", "col"),) * 8
    return jax.shard_map(
        on_device,
        mesh=mesh,
        in_specs=placed,
        out_specs=(P("row", "col"),) * 3,
        check_vma=False,
    )
```

time: 129 us -> 119 us (0.922)
  the two profiles are of different devices: /device:TPU:1 before, /device:TPU:16 now
where the time goes in v2:
time: 119 us; the launch traced here: 118 us
  starting transfers between devices  60.3 us (51%)
  waiting for transfers between devices  24.3 us (20%)
  Pallas kernels  20.2 us (17%)
  local copies, waits for them, and re-layouts  10.8 us (9%)
    ppermute x3, starting transfers between devices, on_device(): down = lax.ppermute(down, 'col', z_shift(-1))  19.3 us
    all_to_all x3, starting transfers between devices, spread(): lax.all_to_all(copies, axis, 0, 0, tiled=True, axis_index_groups=groups)  18.1 us
    all_to_all x3, waiting for transfers between devices, spread(): lax.all_to_all(copies, axis, 0, 0, tiled=True, axis_index_groups=groups)  11.1 us
    ppermute x3, starting transfers between devices, on_device(): up = lax.ppermute(up, 'col', z_shift(1))  10.3 us
    pallas_call x4, Pallas kernels, terms(): pl.pallas_call(functools.partial(term_kernel, len(pieces)), out_shape=(ja...  7.33 us
    all_to_all x1, waiting for transfers between devices, on_device(): parts = lax.all_to_all(local, 'row', 0, 0, tiled=True)  6.32 us
    pallas_call x1, Pallas kernels, below_update(): pl.pallas_call(functools.partial(below_kernel, nb // ZS), grid=(length //...  5.95 us
    ppermute x3, waiting for transfers between devices, on_device(): up = lax.ppermute(up, 'col', z_shift(1))  5.82 us
  transfers between devices with their start and end apart: 12, of which 4 were waited for; matrix products, arithmetic and copies ran while one was open for 5% of the time, Pallas kernels for 13%

profile of v2, /device:TPU:16, one launch (start us, length us, event | category | flops | bytes accessed | tf_op | source)
XLA Modules:
  0.0 117.5 jit_solution(1640600619875778651)
XLA Ops:
  0.6 0.9 select_maximum_fusion
  1.6 0.8 broadcast_in_dim.6
  2.4 9.1 %all-to-all-start = ((f32[4,16,1664]{2,1,0:T(8,128)}), f32[4,16,1664]{2,1,0:T(8,128)S(1)}, u32[]{:S(2)}, u32[]{:S(2)}) async-start(f32[4,16,1664]{2,1,0:T(8,128)} %broadcast_in_dim.6), calls=%async_computation | async-start | bytes 851968 | tf_op jit(solution)/shard_map/all_to_all | solution.py:30
  11.5 11.1 %all-to-all-done = f32[4,16,1664]{2,1,0:T(8,128)S(1)} async-done(((f32[4,16,1664]{2,1,0:T(8,128)}), f32[4,16,1664]{2,1,0:T(8,128)S(1)}, u32[]{:S(2)}, u32[]{:S(2)}) %all-to-all-start) | async-done | bytes 426016 | tf_op jit(solution)/shard_map/all_to_all | solution.py:30
  22.6 0.8 slice.20.refs_0_
  23.4 4.5 %collective-permute-start = (f32[64,1536]{1,0:T(8,128)}, f32[64,1536]{1,0:T(8,128)}, u32[]{:S(2)}, u32[]{:S(2)}) collective-permute-start(f32[64,1536]{1,0:T(8,128)} %slice.20.refs_0_), channel_id=1, source_target_pairs={{0,4},{1,5},{2,6},{3,7},{4,8},{5,9},{6,10},{7,11},{8,12},{9,13},{1... | collective-permute-start | bytes 1179656 | tf_op jit(solution)/shard_map/ppermute | solution.py:225
  27.9 8.6 %collective-permute-start.4 = (f32[64,1536]{1,0:T(8,128)}, f32[64,1536]{1,0:T(8,128)}, u32[]{:S(2)}, u32[]{:S(2)}) collective-permute-start(f32[64,1536]{1,0:T(8,128)} %slice.20.refs_0_), channel_id=1, source_target_pairs={{0,28},{1,29},{2,30},{3,31},{4,0},{5,1},{6,2},{7,3},{8,4},{9,5},{1... | collective-permute-start | bytes 1179656 | tf_op jit(solution)/shard_map/ppermute | solution.py:226
  37.2 4.5 %all-to-all-start.1 = ((f32[8,64,128]{2,1,0:T(8,128)}), f32[8,64,128]{2,1,0:T(8,128)}, u32[]{:S(2)}, u32[]{:S(2)}) async-start(f32[8,64,128]{2,1,0:T(8,128)} %broadcast_in_dim.7), calls=%async_computation.1 | async-start | bytes 524288 | tf_op jit(solution)/shard_map/all_to_all | solution.py:30
  41.7 1.7 %terms.4 = (f32[64,256]{1,0:T(8,128)S(1)}, f32[64,16]{1,0:T(8,128)S(1)}) custom-call(f32[64,1536]{1,0:T(8,128)} %slice.20.refs_0_, f32[1536,256]{1,0:T(8,128)S(1)} %copy-done, f32[16,1536]{1,0:T(8,128)S(1)} %bitcast.11), custom_call_target="tpu_custom_call" | custom-call | flops 199999995904 | tf_op jit(solution)/shard_map/terms/pallas_call | solution.py:65
  44.6 3.9 %collective-permute-start.1 = (f32[64,1536]{1,0:T(8,128)}, f32[64,1536]{1,0:T(8,128)}, u32[]{:S(2)}, u32[]{:S(2)}) collective-permute-start(f32[64,1536]{1,0:T(8,128)} %collective-permute-done.refs_0_.refs_1_), channel_id=1, source_target_pairs={{0,4},{1,5},{2,6},{3,7},{4,8},{5,9},{6,10},{7,11},{8,12},{9,13},{1... | collective-permute-start | bytes 1179656 | tf_op jit(solution)/shard_map/ppermute | solution.py:225
  48.5 1.0 collective-permute-done.4.refs_1_.refs_2_
  49.6 5.6 %collective-permute-start.5 = (f32[64,1536]{1,0:T(8,128)}, f32[64,1536]{1,0:T(8,128)}, u32[]{:S(2)}, u32[]{:S(2)}) collective-permute-start(f32[64,1536]{1,0:T(8,128)} %collective-permute-done.4.refs_1_.refs_2_), channel_id=1, source_target_pairs={{0,28},{1,29},{2,30},{3,31},{4,0},{5,1},{6,2},{7,3},{8,4},{9,5},{1... | collective-permute-start | bytes 1179656 | tf_op jit(solution)/shard_map/ppermute | solution.py:226
  55.2 1.9 %terms.5 = (f32[128,256]{1,0:T(8,128)S(1)}, f32[128,16]{1,0:T(8,128)S(1)}) custom-call(f32[64,1536]{1,0:T(8,128)} %collective-permute-done.refs_0_.refs_1_, f32[64,1536]{1,0:T(8,128)} %collective-permute-done.4.refs_1_.refs_2_, f32[1536,256]{1,0:T(8,128)S(1)} %copy-done, f32[16,1536]{1,0:T(8,128)S(1)} %bitcast.12), custom_call_target="tpu_custom_call" | custom-call | flops 199999995904 | tf_op jit(solution)/shard_map/terms/pallas_call | solution.py:65
  57.1 1.0 slice_bitcast_fusion
  58.2 1.3 %broadcast_in_dim.8 = f32[16,32,768]{2,1,0:T(8,128)} broadcast(f32[32,768]{1,0:T(8,128)S(1)} %pad_maximum_fusion), dimensions={1,2} | broadcast | bytes 1671168 | tf_op jit(solution)/shard_map/broadcast_in_dim | solution.py:29
  59.5 4.4 %all-to-all-start.2 = ((f32[16,32,768]{2,1,0:T(8,128)}), f32[16,32,768]{2,1,0:T(8,128)}, u32[]{:S(2)}, u32[]{:S(2)}) async-start(f32[16,32,768]{2,1,0:T(8,128)} %broadcast_in_dim.8), calls=%async_computation.2 | async-start | bytes 3145728 | tf_op jit(solution)/shard_map/all_to_all | solution.py:30
  63.9 1.9 %collective-permute-start.2 = (f32[64,1536]{1,0:T(8,128)}, f32[64,1536]{1,0:T(8,128)}, u32[]{:S(2)}, u32[]{:S(2)}) collective-permute-start(f32[64,1536]{1,0:T(8,128)} %collective-permute-done.1.refs_0_.refs_3_), channel_id=1, source_target_pairs={{0,4},{1,5},{2,6},{3,7},{4,8},{5,9},{6,10},{7,11},{8,12},{9,13},{1... | collective-permute-start | bytes 1179656 | tf_op jit(solution)/shard_map/ppermute | solution.py:225
  65.9 5.1 %collective-permute-start.6 = (f32[64,1536]{1,0:T(8,128)}, f32[64,1536]{1,0:T(8,128)}, u32[]{:S(2)}, u32[]{:S(2)}) collective-permute-start(f32[64,1536]{1,0:T(8,128)} %collective-permute-done.5.refs_1_.refs_4_), channel_id=1, source_target_pairs={{0,28},{1,29},{2,30},{3,31},{4,0},{5,1},{6,2},{7,3},{8,4},{9,5},{1... | collective-permute-start | bytes 1179656 | tf_op jit(solution)/shard_map/ppermute | solution.py:226
  71.0 1.9 %terms.6 = (f32[128,256]{1,0:T(8,128)S(1)}, f32[128,16]{1,0:T(8,128)S(1)}) custom-call(f32[64,1536]{1,0:T(8,128)} %collective-permute-done.1.refs_0_.refs_3_, f32[64,1536]{1,0:T(8,128)} %collective-permute-done.5.refs_1_.refs_4_, f32[1536,256]{1,0:T(8,128)S(1)} %copy-done, f32[16,1536]{1,0:T(8,128)S(1)} %bitcast.13), custom_call_target="tpu_custom_call" | custom-call | flops 199999995904 | tf_op jit(solution)/shard_map/terms/pallas_call | solution.py:65
  72.9 5.8 %collective-permute-done.2.refs_0_.refs_5_ = f32[64,1536]{1,0:T(8,128)} collective-permute-done((f32[64,1536]{1,0:T(8,128)}, f32[64,1536]{1,0:T(8,128)}, u32[]{:S(2)}, u32[]{:S(2)}) %collective-permute-start.2) | collective-permute-done | bytes 393248 | tf_op jit(solution)/shard_map/ppermute | solution.py:225
  78.7 1.6 %slice.21 = f32[32,1536]{1,0:T(8,128)} slice(f32[64,1536]{1,0:T(8,128)} %collective-permute-done.2.refs_0_.refs_5_), slice={[0:32], [0:1536]} | slice | bytes 393216 | tf_op jit(solution)/shard_map/slice | solution.py:229
  80.4 1.9 %collective-permute-start.3 = (f32[32,1536]{1,0:T(8,128)}, f32[32,1536]{1,0:T(8,128)}, u32[]{:S(2)}, u32[]{:S(2)}) collective-permute-start(f32[32,1536]{1,0:T(8,128)} %slice.21), channel_id=1, source_target_pairs={{0,4},{1,5},{2,6},{3,7},{4,8},{5,9},{6,10},{7,11},{8,12},{9,13},{1... | collective-permute-start | bytes 589832 | tf_op jit(solution)/shard_map/ppermute | solution.py:229
  82.3 1.6 %slice.22 = f32[32,1536]{1,0:T(8,128)} slice(f32[64,1536]{1,0:T(8,128)} %collective-permute-done.6.refs_1_.refs_6_), slice={[32:64], [0:1536]} | slice | bytes 393216 | tf_op jit(solution)/shard_map/slice | solution.py:230
  83.9 5.1 %collective-permute-start.7 = (f32[32,1536]{1,0:T(8,128)}, f32[32,1536]{1,0:T(8,128)}, u32[]{:S(2)}, u32[]{:S(2)}) collective-permute-start(f32[32,1536]{1,0:T(8,128)} %slice.22), channel_id=1, source_target_pairs={{0,28},{1,29},{2,30},{3,31},{4,0},{5,1},{6,2},{7,3},{8,4},{9,5},{1... | collective-permute-start | bytes 589832 | tf_op jit(solution)/shard_map/ppermute | solution.py:230
  89.0 1.9 %terms.7 = (f32[128,256]{1,0:T(8,128)S(1)}, f32[128,16]{1,0:T(8,128)S(1)}) custom-call(f32[64,1536]{1,0:T(8,128)} %collective-permute-done.2.refs_0_.refs_5_, f32[64,1536]{1,0:T(8,128)} %collective-permute-done.6.refs_1_.refs_6_, f32[1536,256]{1,0:T(8,128)S(1)} %copy-done, f32[16,1536]{1,0:T(8,128)S(1)} %bitcast.14), custom_call_target="tpu_custom_call" | custom-call | flops 199999995904 | tf_op jit(solution)/shard_map/terms/pallas_call | solution.py:65
  91.0 2.1 %weights.1 = (f32[512,256]{1,0:T(8,128)S(1)}, bf16[512,512]{1,0:T(8,128)(2,1)S(1)}, bf16[512,512]{1,0:T(8,128)(2,1)S(1)}) custom-call(f32[512,768]{1,0:T(8,128)} %bitcast.7.packed_ref), custom_call_target="tpu_custom_call" | custom-call | flops 1000000000 | tf_op jit(solution)/shard_map/weights/pallas_call | solution.py:85
  93.1 0.8 copy-done.2
  94.0 0.8 copy-done.13
  94.8 4.1 %head_terms.1 = f32[16,40,256]{2,1,0:T(8,128)} custom-call(s32[1]{0:T(128)} %bitcast.z_ref, f32[32,1536]{1,0:T(8,128)} %collective-permute-done.3.refs_0_.refs_7_, f32[32,1536]{1,0:T(8,128)} %collective-permute-done.7.refs_1_.refs_8_, f32[1536,256]{1,0:T(8,128)S(1)} %copy-done, f32[16,1536]{1,0:T(8,128)S(1)} %bitcast.15, ...), custom_call_target="tpu_custom_call" | custom-call | flops 1000000000 | tf_op jit(solution)/shard_map/head_terms/pallas_call | solution.py:129
  98.9 5.6 %all-to-all-start.3 = ((f32[16,40,256]{2,1,0:T(8,128)}), f32[16,40,256]{2,1,0:T(8,128)S(1)}, u32[]{:S(2)}, u32[]{:S(2)}) async-start(f32[16,40,256]{2,1,0:T(8,128)} %head_terms.1), calls=%async_computation.3 | async-start | bytes 1310720 | tf_op jit(solution)/shard_map/all_to_all | solution.py:236
  104.5 5.9 %below_update.1 = f32[1536,256]{1,0:T(8,128)} custom-call(s32[1]{0:T(128)} %bitcast.z_ref, f32[64,1536]{1,0:T(8,128)} %slice.20.refs_0_, f32[64,1536]{1,0:T(8,128)} %collective-permute-done.refs_0_.refs_1_, f32[64,1536]{1,0:T(8,128)} %collective-permute-done.4.refs_1_.refs_2_, f32[64,1536]{1,0:T(8,128)} %collective-permute-done.1.refs_0_.refs_3_, ...), custom_call_target="tpu_custom_call" | custom-call | flops 1207959552 | tf_op jit(solution)/shard_map/below_update/pallas_call | solution.py:160
  110.4 6.3 %all-to-all-done.3.parts_ref = f32[16,40,256]{2,1,0:T(8,128)S(1)} async-done(((f32[16,40,256]{2,1,0:T(8,128)}), f32[16,40,256]{2,1,0:T(8,128)S(1)}, u32[]{:S(2)}, u32[]{:S(2)}) %all-to-all-start.3) | async-done | bytes 655392 | tf_op jit(solution)/shard_map/all_to_all | solution.py:236
  (49 shorter events, 2.9 us)
Async XLA Ops:
  1.5 40.1 %copy-start = (f32[1536,256]{1,0:T(8,128)S(1)}, f32[1536,256]{1,0:T(8,128)}, u32[]{:S(2)}) copy-start(f32[1536,256]{1,0:T(8,128)} %refs_2_.7) | copy-start | bytes 4718596
  1.6 40.1 %copy-start.4 = (f32[1536,16]{0,1:T(8,128)S(1)}, f32[1536,16]{0,1:T(8,128)}, u32[]{:S(2)}) copy-start(f32[1536,16]{0,1:T(8,128)} %param.9) | copy-start | bytes 294916
  2.4 20.2 %all-to-all-start = ((f32[4,16,1664]{2,1,0:T(8,128)}), f32[4,16,1664]{2,1,0:T(8,128)S(1)}, u32[]{:S(2)}, u32[]{:S(2)}) async-start(f32[4,16,1664]{2,1,0:T(8,128)} %broadcast_in_dim.6), calls=%async_computation | async-start | bytes 851968 | tf_op jit(solution)/shard_map/all_to_all | solution.py:30
  23.4 21.2 %collective-permute-start = (f32[64,1536]{1,0:T(8,128)}, f32[64,1536]{1,0:T(8,128)}, u32[]{:S(2)}, u32[]{:S(2)}) collective-permute-start(f32[64,1536]{1,0:T(8,128)} %slice.20.refs_0_), channel_id=1, source_target_pairs={{0,4},{1,5},{2,6},{3,7},{4,8},{5,9},{6,10},{7,11},{8,12},{9,13},{1... | collective-permute-start | bytes 1179656 | tf_op jit(solution)/shard_map/ppermute | solution.py:225
  27.9 21.7 %collective-permute-start.4 = (f32[64,1536]{1,0:T(8,128)}, f32[64,1536]{1,0:T(8,128)}, u32[]{:S(2)}, u32[]{:S(2)}) collective-permute-start(f32[64,1536]{1,0:T(8,128)} %slice.20.refs_0_), channel_id=1, source_target_pairs={{0,28},{1,29},{2,30},{3,31},{4,0},{5,1},{6,2},{7,3},{8,4},{9,5},{1... | collective-permute-start | bytes 1179656 | tf_op jit(solution)/shard_map/ppermute | solution.py:226
  37.2 19.9 %all-to-all-start.1 = ((f32[8,64,128]{2,1,0:T(8,128)}), f32[8,64,128]{2,1,0:T(8,128)}, u32[]{:S(2)}, u32[]{:S(2)}) async-start(f32[8,64,128]{2,1,0:T(8,128)} %broadcast_in_dim.7), calls=%async_computation.1 | async-start | bytes 524288 | tf_op jit(solution)/shard_map/all_to_all | solution.py:30
  43.4 0.6 copy-start.6
  44.0 0.6 copy-start.14
  44.6 19.3 %collective-permute-start.1 = (f32[64,1536]{1,0:T(8,128)}, f32[64,1536]{1,0:T(8,128)}, u32[]{:S(2)}, u32[]{:S(2)}) collective-permute-start(f32[64,1536]{1,0:T(8,128)} %collective-permute-done.refs_0_.refs_1_), channel_id=1, source_target_pairs={{0,4},{1,5},{2,6},{3,7},{4,8},{5,9},{6,10},{7,11},{8,12},{9,13},{1... | collective-permute-start | bytes 1179656 | tf_op jit(solution)/shard_map/ppermute | solution.py:225
  49.6 16.3 %collective-permute-start.5 = (f32[64,1536]{1,0:T(8,128)}, f32[64,1536]{1,0:T(8,128)}, u32[]{:S(2)}, u32[]{:S(2)}) collective-permute-start(f32[64,1536]{1,0:T(8,128)} %collective-permute-done.4.refs_1_.refs_2_), channel_id=1, source_target_pairs={{0,28},{1,29},{2,30},{3,31},{4,0},{5,1},{6,2},{7,3},{8,4},{9,5},{1... | collective-permute-start | bytes 1179656 | tf_op jit(solution)/shard_map/ppermute | solution.py:226
  55.1 3.0 %copy-start.18 = (f32[32,256]{1,0:T(8,128)S(1)}, f32[32,256]{1,0:T(8,128)}, u32[]{:S(2)}) copy-start(f32[32,256]{1,0:T(8,128)} %param.11) | copy-start | bytes 98308
  57.0 2.4 %copy-start.8 = (f32[128,16]{1,0:T(8,128)}, f32[128,16]{1,0:T(8,128)S(1)}, u32[]{:S(2)}) copy-start(f32[128,16]{1,0:T(8,128)S(1)} %get-tuple-element.21.refs_9_) | copy-start | bytes 24580
  59.5 31.5 %all-to-all-start.2 = ((f32[16,32,768]{2,1,0:T(8,128)}), f32[16,32,768]{2,1,0:T(8,128)}, u32[]{:S(2)}, u32[]{:S(2)}) async-start(f32[16,32,768]{2,1,0:T(8,128)} %broadcast_in_dim.8), calls=%async_computation.2 | async-start | bytes 3145728 | tf_op jit(solution)/shard_map/all_to_all | solution.py:30
  63.9 14.8 %collective-permute-start.2 = (f32[64,1536]{1,0:T(8,128)}, f32[64,1536]{1,0:T(8,128)}, u32[]{:S(2)}, u32[]{:S(2)}) collective-permute-start(f32[64,1536]{1,0:T(8,128)} %collective-permute-done.1.refs_0_.refs_3_), channel_id=1, source_target_pairs={{0,4},{1,5},{2,6},{3,7},{4,8},{5,9},{6,10},{7,11},{8,12},{9,13},{1... | collective-permute-start | bytes 1179656 | tf_op jit(solution)/shard_map/ppermute | solution.py:225
  65.9 16.4 %collective-permute-start.6 = (f32[64,1536]{1,0:T(8,128)}, f32[64,1536]{1,0:T(8,128)}, u32[]{:S(2)}, u32[]{:S(2)}) collective-permute-start(f32[64,1536]{1,0:T(8,128)} %collective-permute-done.5.refs_1_.refs_4_), channel_id=1, source_target_pairs={{0,28},{1,29},{2,30},{3,31},{4,0},{5,1},{6,2},{7,3},{8,4},{9,5},{1... | collective-permute-start | bytes 1179656 | tf_op jit(solution)/shard_map/ppermute | solution.py:226
  72.9 18.0 %copy-start.10 = (f32[128,16]{1,0:T(8,128)}, f32[128,16]{1,0:T(8,128)S(1)}, u32[]{:S(2)}) copy-start(f32[128,16]{1,0:T(8,128)S(1)} %get-tuple-element.23.refs_11_) | copy-start | bytes 24580
  80.4 13.6 %collective-permute-start.3 = (f32[32,1536]{1,0:T(8,128)}, f32[32,1536]{1,0:T(8,128)}, u32[]{:S(2)}, u32[]{:S(2)}) collective-permute-start(f32[32,1536]{1,0:T(8,128)} %slice.21), channel_id=1, source_target_pairs={{0,4},{1,5},{2,6},{3,7},{4,8},{5,9},{6,10},{7,11},{8,12},{9,13},{1... | collective-permute-start | bytes 589832 | tf_op jit(solution)/shard_map/ppermute | solution.py:229
  83.9 10.0 %collective-permute-start.7 = (f32[32,1536]{1,0:T(8,128)}, f32[32,1536]{1,0:T(8,128)}, u32[]{:S(2)}, u32[]{:S(2)}) collective-permute-start(f32[32,1536]{1,0:T(8,128)} %slice.22), channel_id=1, source_target_pairs={{0,28},{1,29},{2,30},{3,31},{4,0},{5,1},{6,2},{7,3},{8,4},{9,5},{1... | collective-permute-start | bytes 589832 | tf_op jit(solution)/shard_map/ppermute | solution.py:230
  90.9 2.2 %copy-start.12 = (f32[128,16]{1,0:T(8,128)}, f32[128,16]{1,0:T(8,128)S(1)}, u32[]{:S(2)}) copy-start(f32[128,16]{1,0:T(8,128)S(1)} %get-tuple-element.25.refs_13_) | copy-start | bytes 24580
  91.0 3.0 %copy-start.5 = (f32[1536,16]{0,1:T(8,128)S(1)}, f32[1536,16]{0,1:T(8,128)}, u32[]{:S(2)}) copy-start(f32[1536,16]{0,1:T(8,128)} %param.9) | copy-start | bytes 294916
  91.0 3.0 %copy-start.7 = (f32[64,256]{1,0:T(8,128)S(1)}, f32[64,256]{1,0:T(8,128)}, u32[]{:S(2)}) copy-start(f32[64,256]{1,0:T(8,128)} %copy-done.6) | copy-start | bytes 196612
  91.0 3.0 %copy-start.9 = (f32[128,16]{1,0:T(8,128)S(1)}, f32[128,16]{1,0:T(8,128)}, u32[]{:S(2)}) copy-start(f32[128,16]{1,0:T(8,128)} %copy-done.8) | copy-start | bytes 24580
  91.0 3.0 %copy-start.11 = (f32[128,16]{1,0:T(8,128)S(1)}, f32[128,16]{1,0:T(8,128)}, u32[]{:S(2)}) copy-start(f32[128,16]{1,0:T(8,128)} %copy-done.10) | copy-start | bytes 24580
  91.0 3.0 %copy-start.15 = (f32[64,16]{1,0:T(8,128)S(1)}, f32[64,16]{1,0:T(8,128)}, u32[]{:S(2)}) copy-start(f32[64,16]{1,0:T(8,128)} %copy-done.14) | copy-start | bytes 12292
  93.1 0.8 copy-start.2
  94.0 0.8 copy-start.13
  94.8 9.7 %copy-start.1 = (f32[1536,256]{1,0:T(8,128)S(1)}, f32[1536,256]{1,0:T(8,128)}, u32[]{:S(2)}) copy-start(f32[1536,256]{1,0:T(8,128)} %refs_10_.1) | copy-start | bytes 4718596
  98.9 5.6 %copy-start.3 = (f32[512,256]{1,0:T(8,128)S(1)}, f32[512,256]{1,0:T(8,128)}, u32[]{:S(2)}) copy-start(f32[512,256]{1,0:T(8,128)} %copy-done.2) | copy-start | bytes 1572868
  98.9 17.9 %all-to-all-start.3 = ((f32[16,40,256]{2,1,0:T(8,128)}), f32[16,40,256]{2,1,0:T(8,128)S(1)}, u32[]{:S(2)}, u32[]{:S(2)}) async-start(f32[16,40,256]{2,1,0:T(8,128)} %head_terms.1), calls=%async_computation.3 | async-start | bytes 1310720 | tf_op jit(solution)/shard_map/all_to_all | solution.py:236
  104.5 12.3 %copy-start.16 = (f32[32,256]{1,0:T(8,128)S(1)}, f32[32,256]{1,0:T(8,128)}, u32[]{:S(2)}) copy-start(f32[32,256]{1,0:T(8,128)} %head_ref.1) | copy-start | bytes 98308
  104.5 12.3 %copy-start.17 = (f32[32,16]{0,1:T(8,128)S(1)}, f32[32,16]{0,1:T(8,128)}, u32[]{:S(2)}) copy-start(f32[32,16]{0,1:T(8,128)} %param.13) | copy-start | bytes 6148

commit v3 on v2

--- a/solution.py
+++ b/solution.py
@@ -11,7 +11,7 @@
 YS = 4
 RS = 16
 TILE = 256
-FLOPS = 20 * 10**10
+COSTS = (2 * 10**11,) * 4
 VMEM = 14 * 2**20
 
 
@@ -21,12 +21,16 @@
     return near, far
 
 
-def z_shift(step):
-    return [(z * YS + h, ((z + step) % ZS) * YS + h) for z in range(ZS) for h in range(YS)]
-
-
-def spread(block, axis, groups, size):
-    copies = jnp.broadcast_to(block[None], (size,) + block.shape)
+def along_z(step):
+    moves = []
+    for r in range(RS):
+        for z in range(ZS):
+            to = (z + (step if r % 2 == 0 else -step)) % ZS
+            moves += [((r * ZS + z) * YS + h, (r * ZS + to) * YS + h) for h in range(YS)]
+    return moves
+
+
+def exchange(copies, axis, groups):
     return lax.all_to_all(copies, axis, 0, 0, tiled=True, axis_index_groups=groups)
 
 
@@ -60,7 +64,7 @@
     return pltpu.CompilerParams(vmem_limit_bytes=VMEM, **more)
 
 
-def terms(pieces, b, f):
+def terms(pieces, b, f, cost):
     rows = sum(p.shape[0] for p in pieces)
     return pl.pallas_call(
         functools.partial(term_kernel, len(pieces)),
@@ -69,49 +73,45 @@
             jax.ShapeDtypeStruct((rows, f.shape[0]), jnp.float32),
         ),
         compiler_params=params(),
-        cost_estimate=pl.CostEstimate(flops=FLOPS, bytes_accessed=0, transcendentals=0),
+        cost_estimate=pl.CostEstimate(flops=cost, bytes_accessed=0, transcendentals=0),
         name="terms",
     )(*pieces, b, f)
 
 
-def weight_kernel(width, packed_ref, w_ref, high_ref, low_ref):
-    inverse = packed_ref[:, width:]
-    w_ref[...] = dot3(split(inverse), split(packed_ref[:, :width]), ((1,), (0,)))
-    high_ref[...], low_ref[...] = split(inverse.T)
+def weight_kernel(width, packed_ref, w_ref):
+    inverse = split(packed_ref[:, width:])
+    w_ref[...] = dot3(inverse, split(packed_ref[:, :width]), ((1,), (0,)))
 
 
 def weights(packed, width):
     nb = packed.shape[0]
     return pl.pallas_call(
         functools.partial(weight_kernel, width),
-        out_shape=(
-            jax.ShapeDtypeStruct((nb, width), jnp.float32),
-            jax.ShapeDtypeStruct((nb, nb), jnp.bfloat16),
-            jax.ShapeDtypeStruct((nb, nb), jnp.bfloat16),
-        ),
+        out_shape=jax.ShapeDtypeStruct((nb, width), jnp.float32),
         compiler_params=params(),
         cost_estimate=pl.CostEstimate(flops=10**9, bytes_accessed=0, transcendentals=0),
         name="weights",
     )(packed)
 
 
+def position(z_ref, offset, group):
+    place = lax.rem(z_ref[0] + offset * z_ref[1] + ZS, ZS)
+    return pl.ds(pl.multiple_of(place * group, group), group)
+
+
 def head_kernel(group, z_ref, *refs):
-    up_ref, down_ref, b_ref, f_ref, high_ref, low_ref = refs[:6]
-    found = refs[6:14]
-    out_ref, t_scr, s_scr = refs[14:]
-    z = z_ref[0]
-
-    def place(offset):
-        return pl.ds(pl.multiple_of(lax.rem(z + offset + ZS, ZS) * group, group), group)
-
+    piece_ref, b_ref, f_ref, packed_ref = refs[:4]
+    found = refs[4:12]
+    out_ref, t_scr, s_scr = refs[12:]
+    turned = split(packed_ref[:, b_ref.shape[1] :].T)
     for step in range(ZS // 2):
         t_ref, s_ref = found[2 * step], found[2 * step + 1]
-        for part, offset in enumerate((0,) if step == 0 else (-step, step)):
-            t_scr[place(offset), :] = t_ref[part * group : (part + 1) * group, :]
-            s_scr[place(offset), :] = s_ref[part * group : (part + 1) * group, :]
-    last = place(ZS // 2)
-    t_scr[last, :], s_scr[last, :] = products(joined((up_ref, down_ref)), b_ref, f_ref)
-    turned = (high_ref[...], low_ref[...])
+        for part, offset in enumerate((0,) if step == 0 else (step, -step)):
+            place = position(z_ref, offset, group)
+            t_scr[place, :] = t_ref[part * group : (part + 1) * group, :]
+            s_scr[place, :] = s_ref[part * group : (part + 1) * group, :]
+    last = position(z_ref, ZS // 2, group)
+    t_scr[last, :], s_scr[last, :] = products(piece_ref[...], b_ref, f_ref)
     head = dot3(turned, split(t_scr[...]), ((1,), (0,)))
     diag = dot3(turned, split(s_scr[...]), ((1,), (0,)))
     rows = head.shape[0] // RS
@@ -122,10 +122,10 @@
             out_ref[r, rows:, q * 64 : q * 64 + small] = diag[r * rows + q * 8 : r * rows + q * 8 + 8]
 
 
-def head_terms(z, up, down, b, f, turned, found):
-    nb = turned[0].shape[0]
+def head_terms(z, piece, b, f, packed, found):
+    nb = packed.shape[0]
     width, small = b.shape[1], f.shape[0]
-    args = (up, down, b, f) + turned + found
+    args = (piece, b, f, packed) + found
     return pl.pallas_call(
         functools.partial(head_kernel, nb // ZS),
         out_shape=jax.ShapeDtypeStruct((RS, nb // RS + 8, width), jnp.float32),
@@ -140,16 +140,9 @@
 
 
 def below_kernel(group, z_ref, *refs):
-    pieces, (w_ref, old_ref, new_ref) = refs[:9], refs[9:]
-    z = z_ref[0]
-    order = (0, -1, 1, -2, 2, -3, 3, 4)
-    weight = jnp.concatenate(
-        [
-            w_ref[pl.ds(pl.multiple_of(lax.rem(z + k + ZS, ZS) * group, group), group), :]
-            for k in order
-        ],
-        0,
-    )
+    pieces, (w_ref, old_ref, new_ref) = refs[:-3], refs[-3:]
+    order = (0, 1, -1, 2, -2, 3, -3, 4)
+    weight = jnp.concatenate([w_ref[position(z_ref, k, group), :] for k in order], 0)
     panel = joined(pieces)
     new_ref[...] = old_ref[...] - dot3(split(panel), split(weight), ((0,), (0,)))
 
@@ -196,6 +189,26 @@
         compiler_params=params(),
         name="finish",
     )(parts, head, diag)
+
+
+def packed_kernel(head_ref, inverse_ref, out_ref):
+    rows, width = head_ref.shape
+    inverse = inverse_ref[...].T[:rows]
+    for k in range(RS):
+        out_ref[k, :, :width] = head_ref[...]
+        out_ref[k, :, width:] = inverse
+
+
+def packed_copies(head, inverse):
+    rows, width = head.shape
+    nb = inverse.shape[0]
+    return pl.pallas_call(
+        packed_kernel,
+        out_shape=jax.ShapeDtypeStruct((RS, rows, width + nb), jnp.float32),
+        compiler_params=params(),
+        cost_estimate=pl.CostEstimate(flops=10**8, bytes_accessed=0, transcendentals=0),
+        name="packed_copies",
+    )(head, inverse)
 
 
 def on_device(
@@ -209,30 +222,34 @@
     below_adjoint,
 ):
     near, far = col_groups()
-    z = (lax.axis_index("col") // YS).astype(jnp.int32).reshape(1)
-    rows, width = head_factor.shape
+    turn = 2 * (lax.axis_index("row") % 2) - 1
+    z = jnp.stack([lax.axis_index("col") // YS, turn]).astype(jnp.int32)
+    width = head_factor.shape[1]
     length, cols = panel_adjoint.shape
     nb = cols * ZS * YS
     group = cols * YS
     factor = panel_factor.T
-    corner = jnp.pad(diag_inverse.T, ((0, 0), (0, 128 - rows)))
-    part = spread(jnp.concatenate([panel_adjoint.T, corner], 1), "col", near, YS)
+    corner = jnp.pad(diag_inverse.T, ((0, 0), (0, 128 - head_factor.shape[0])))
+    part = jnp.concatenate([panel_adjoint.T, corner], 1)
+    part = exchange(jnp.broadcast_to(part[None], (YS,) + part.shape), "col", near)
     part = part.reshape(group, length + 128)
-    up = down = part[:, :length]
-    pieces = [up]
-    found = terms((up,), below_factor, factor)
+    inverse = jnp.broadcast_to(part[None, :, length:], (ZS, group, 128))
+    inverse = exchange(inverse, "col", far).reshape(nb, 128)
+    copies, later_factor = lax.optimization_barrier((packed_copies(head_factor, inverse), below_factor))
+    packed = exchange(copies, "row", None).reshape(nb, width + nb)
+    one = other = part[:, :length]
+    pieces = [one]
+    found = terms((one,), below_factor, factor, COSTS[0])
     for step in range(1, ZS // 2):
-        up = lax.ppermute(up, "col", z_shift(1))
-        down = lax.ppermute(down, "col", z_shift(-1))
-        found += tuple(terms((up, down), below_factor, factor))
-        pieces += [up, down]
-    up = lax.ppermute(up[: group // 2], "col", z_shift(1))
-    down = lax.ppermute(down[group // 2 :], "col", z_shift(-1))
-    pieces += [up, down]
-    inverse = spread(part[:, length:], "col", far, ZS).reshape(nb, 128)[:, :rows]
-    packed = spread(jnp.concatenate([head_factor, inverse.T], 1), "row", None, RS)
-    weight, high, low = weights(packed.reshape(nb, width + nb), width)
-    local = head_terms(z, up, down, below_factor, factor, (high, low), tuple(found))
+        one = lax.ppermute(one, ("row", "col"), along_z(1))
+        other = lax.ppermute(other, ("row", "col"), along_z(-1))
+        found += tuple(terms((one, other), later_factor, factor, COSTS[step]))
+        pieces += [one, other]
+    one = lax.ppermute(one, ("row", "col"), along_z(1))
+    pieces.append(one)
+    local = head_terms(z, one, later_factor, factor, packed, tuple(found))
+    packed, local = lax.optimization_barrier((packed, local))
+    weight = weights(packed, width)
     parts = lax.all_to_all(local, "row", 0, 0, tiled=True)
     below_updated = below_update(z, pieces, weight, below_adjoint)
     head_updated, diag_updated = finish(parts, head_adjoint, diag_adjoint.T)

time: 119 us -> 111 us (0.933)
  local copies, waits for them, and re-layouts: 10.8 us -> 2.32 us
  starting transfers between devices: 60.3 us -> 54.4 us
  waiting for transfers between devices: 24.3 us -> 28.7 us
  Pallas kernels: 20.2 us -> 22.9 us
    ppermute x8 -> x7, starting transfers between devices: 36.6 us -> 30.5 us  [the longest x3 17.2 us: on_device(): other = lax.ppermute(other, ('row', 'col'), along_z(-1))]
    ppermute x8 -> x7, waiting for transfers between devices: 6.86 us -> 12.4 us  [the longest x4 12.4 us: on_device(): one = lax.ppermute(one, ('row', 'col'), along_z(1))]
    slice x4 -> x2, local copies, waits for them, and re-layouts: 4.01 us -> 0.78 us  [the longest x1 0.78 us: on_device(): one = other = part[:, :length]]
    unnamed x38 -> x12, local copies, waits for them, and re-layouts: 2.93 us -> 0.04 us
    pallas_call x1 -> x2, Pallas kernels: 2.09 us -> 4.37 us  [the longest x1 2.26 us: packed_copies(): pl.pallas_call(packed_kernel, out_shape=jax.ShapeDtypeStruct((RS, rows, w...]
    all_to_all x1, waiting for transfers between devices: 6.32 us -> 4.1 us  [on_device(): parts = lax.all_to_all(local, 'row', 0, 0, tiled=True)]
    broadcast_in_dim x3 -> x2, local copies, waits for them, and re-layouts: 2.8 us -> 1.51 us  [the longest x1 0.79 us: on_device(): jnp.broadcast_to(part[None], (YS,) + part.shape)]
  transfers between devices with their start and end apart: 12 -> 11, of which waited for: 4 -> 5; matrix products, arithmetic and copies ran while one was open for 5% -> 1% of each run, Pallas kernels for 13% -> 16%
where the time goes in v3:
time: 111 us; the launch traced here: 110 us
  starting transfers between devices  54.4 us (49%)
  waiting for transfers between devices  28.7 us (26%)
  Pallas kernels  22.9 us (21%)
  local copies, waits for them, and re-layouts  2.32 us (2%)
    all_to_all x3, starting transfers between devices, exchange(): lax.all_to_all(copies, axis, 0, 0, tiled=True, axis_index_groups=groups)  18.1 us
    ppermute x3, starting transfers between devices, on_device(): other = lax.ppermute(other, ('row', 'col'), along_z(-1))  17.2 us
    ppermute x4, starting transfers between devices, on_device(): one = lax.ppermute(one, ('row', 'col'), along_z(1))  13.3 us
    ppermute x4, waiting for transfers between devices, on_device(): one = lax.ppermute(one, ('row', 'col'), along_z(1))  12.4 us
    all_to_all x3, waiting for transfers between devices, exchange(): lax.all_to_all(copies, axis, 0, 0, tiled=True, axis_index_groups=groups)  12.2 us
    pallas_call x4, Pallas kernels, terms(): pl.pallas_call(functools.partial(term_kernel, len(pieces)), out_shape=(ja...  7.33 us
    pallas_call x1, Pallas kernels, below_update(): pl.pallas_call(functools.partial(below_kernel, nb // ZS), grid=(length //...  6.05 us
    all_to_all x1, starting transfers between devices, on_device(): parts = lax.all_to_all(local, 'row', 0, 0, tiled=True)  5.91 us
  transfers between devices with their start and end apart: 11, of which 5 were waited for; matrix products, arithmetic and copies ran while one was open for 1% of the time, Pallas kernels for 16%

profile of v3, /device:TPU:16, one launch (start us, length us, event | category | flops | bytes accessed | tf_op | source)
XLA Modules:
  0.0 110.2 jit_solution(11343721949386223037)
XLA Ops:
  0.6 0.9 select_maximum_fusion
  1.6 0.0 copy-start.2
  1.6 0.8 broadcast_in_dim.4
  2.4 9.1 %all-to-all-start = ((f32[4,16,1664]{2,1,0:T(8,128)}), f32[4,16,1664]{2,1,0:T(8,128)S(1)}, u32[]{:S(2)}, u32[]{:S(2)}) async-start(f32[4,16,1664]{2,1,0:T(8,128)} %broadcast_in_dim.4), calls=%async_computation | async-start | bytes 851968 | tf_op jit(solution)/shard_map/all_to_all | solution.py:34
  11.5 0.1 pad_add_fusion.z_ref
  11.6 11.0 %all-to-all-done = f32[4,16,1664]{2,1,0:T(8,128)S(1)} async-done(((f32[4,16,1664]{2,1,0:T(8,128)}), f32[4,16,1664]{2,1,0:T(8,128)S(1)}, u32[]{:S(2)}, u32[]{:S(2)}) %all-to-all-start) | async-done | bytes 426016 | tf_op jit(solution)/shard_map/all_to_all | solution.py:34
  22.6 0.8 slice.9.refs_0_
  23.4 4.5 %collective-permute-start = (f32[64,1536]{1,0:T(8,128)}, f32[64,1536]{1,0:T(8,128)}, u32[]{:S(2)}, u32[]{:S(2)}) collective-permute-start(f32[64,1536]{1,0:T(8,128)} %slice.9.refs_0_), channel_id=1, source_target_pairs={{0,4},{1,5},{2,6},{3,7},{4,8},{5,9},{6,10},{7,11},{8,12},{9,13},{1... | collective-permute-start | bytes 1179656 | tf_op jit(solution)/shard_map/ppermute | solution.py:244
  27.9 8.6 %collective-permute-start.4 = (f32[64,1536]{1,0:T(8,128)}, f32[64,1536]{1,0:T(8,128)}, u32[]{:S(2)}, u32[]{:S(2)}) collective-permute-start(f32[64,1536]{1,0:T(8,128)} %slice.9.refs_0_), channel_id=1, source_target_pairs={{0,28},{1,29},{2,30},{3,31},{4,0},{5,1},{6,2},{7,3},{8,4},{9,5},{1... | collective-permute-start | bytes 1179656 | tf_op jit(solution)/shard_map/ppermute | solution.py:245
  36.5 0.7 broadcast_in_dim.5
  37.2 4.5 %all-to-all-start.1 = ((f32[8,64,128]{2,1,0:T(8,128)}), f32[8,64,128]{2,1,0:T(8,128)}, u32[]{:S(2)}, u32[]{:S(2)}) async-start(f32[8,64,128]{2,1,0:T(8,128)} %broadcast_in_dim.5), calls=%async_computation.1 | async-start | bytes 524288 | tf_op jit(solution)/shard_map/all_to_all | solution.py:34
  41.7 1.7 %terms.4 = (f32[64,256]{1,0:T(8,128)S(1)}, f32[64,16]{1,0:T(8,128)S(1)}) custom-call(f32[64,1536]{1,0:T(8,128)} %slice.9.refs_0_, f32[1536,256]{1,0:T(8,128)S(1)} %copy-done, f32[16,1536]{1,0:T(8,128)S(1)} %bitcast.10), custom_call_target="tpu_custom_call" | custom-call | flops 199999995904 | tf_op jit(solution)/shard_map/terms/pallas_call | solution.py:69
  43.4 3.9 %collective-permute-start.1 = (f32[64,1536]{1,0:T(8,128)}, f32[64,1536]{1,0:T(8,128)}, u32[]{:S(2)}, u32[]{:S(2)}) collective-permute-start(f32[64,1536]{1,0:T(8,128)} %collective-permute-done.refs_0_.refs_1_), channel_id=1, source_target_pairs={{0,4},{1,5},{2,6},{3,7},{4,8},{5,9},{6,10},{7,11},{8,12},{9,13},{1... | collective-permute-start | bytes 1179656 | tf_op jit(solution)/shard_map/ppermute | solution.py:244
  47.3 4.5 %collective-permute-start.5 = (f32[64,1536]{1,0:T(8,128)}, f32[64,1536]{1,0:T(8,128)}, u32[]{:S(2)}, u32[]{:S(2)}) collective-permute-start(f32[64,1536]{1,0:T(8,128)} %collective-permute-done.4.refs_1_.refs_2_), channel_id=1, source_target_pairs={{0,28},{1,29},{2,30},{3,31},{4,0},{5,1},{6,2},{7,3},{8,4},{9,5},{1... | collective-permute-start | bytes 1179656 | tf_op jit(solution)/shard_map/ppermute | solution.py:245
  51.8 1.1 %all-to-all-done.1 = f32[8,64,128]{2,1,0:T(8,128)} async-done(((f32[8,64,128]{2,1,0:T(8,128)}), f32[8,64,128]{2,1,0:T(8,128)}, u32[]{:S(2)}, u32[]{:S(2)}) %all-to-all-start.1) | async-done | bytes 262176 | tf_op jit(solution)/shard_map/all_to_all | solution.py:34
  53.0 2.3 %packed_copies.1 = f32[16,32,768]{2,1,0:T(8,128)} custom-call(f32[32,256]{1,0:T(8,128)S(1)} %copy-done.3, f32[512,128]{1,0:T(8,128)} %bitcast.3.inverse_ref), custom_call_target="tpu_custom_call" | custom-call | flops 100000000 | tf_op jit(solution)/shard_map/packed_copies/pallas_call | solution.py:205
  55.2 4.4 %all-to-all-start.2 = ((f32[16,32,768]{2,1,0:T(8,128)}), f32[16,32,768]{2,1,0:T(8,128)}, u32[]{:S(2)}, u32[]{:S(2)}) async-start(f32[16,32,768]{2,1,0:T(8,128)} %packed_copies.1), calls=%async_computation.2 | async-start | bytes 3145728 | tf_op jit(solution)/shard_map/all_to_all | solution.py:34
  59.7 1.9 %terms.5 = (f32[128,256]{1,0:T(8,128)S(1)}, f32[128,16]{1,0:T(8,128)S(1)}) custom-call(f32[64,1536]{1,0:T(8,128)} %collective-permute-done.refs_0_.refs_1_, f32[64,1536]{1,0:T(8,128)} %collective-permute-done.4.refs_1_.refs_2_, f32[1536,256]{1,0:T(8,128)S(1)} %copy-done, f32[16,1536]{1,0:T(8,128)S(1)} %bitcast.11), custom_call_target="tpu_custom_call" | custom-call | flops 199999995904 | tf_op jit(solution)/shard_map/terms/pallas_call | solution.py:69
  61.6 3.0 %collective-permute-start.2 = (f32[64,1536]{1,0:T(8,128)}, f32[64,1536]{1,0:T(8,128)}, u32[]{:S(2)}, u32[]{:S(2)}) collective-permute-start(f32[64,1536]{1,0:T(8,128)} %collective-permute-done.1.refs_0_.refs_3_), channel_id=1, source_target_pairs={{0,4},{1,5},{2,6},{3,7},{4,8},{5,9},{6,10},{7,11},{8,12},{9,13},{1... | collective-permute-start | bytes 1179656 | tf_op jit(solution)/shard_map/ppermute | solution.py:244
  64.6 4.1 %collective-permute-start.6 = (f32[64,1536]{1,0:T(8,128)}, f32[64,1536]{1,0:T(8,128)}, u32[]{:S(2)}, u32[]{:S(2)}) collective-permute-start(f32[64,1536]{1,0:T(8,128)} %collective-permute-done.5.refs_1_.refs_4_), channel_id=1, source_target_pairs={{0,28},{1,29},{2,30},{3,31},{4,0},{5,1},{6,2},{7,3},{8,4},{9,5},{1... | collective-permute-start | bytes 1179656 | tf_op jit(solution)/shard_map/ppermute | solution.py:245
  68.7 1.9 %terms.6 = (f32[128,256]{1,0:T(8,128)S(1)}, f32[128,16]{1,0:T(8,128)S(1)}) custom-call(f32[64,1536]{1,0:T(8,128)} %collective-permute-done.1.refs_0_.refs_3_, f32[64,1536]{1,0:T(8,128)} %collective-permute-done.5.refs_1_.refs_4_, f32[1536,256]{1,0:T(8,128)S(1)} %copy-done, f32[16,1536]{1,0:T(8,128)S(1)} %bitcast.12), custom_call_target="tpu_custom_call" | custom-call | flops 199999995904 | tf_op jit(solution)/shard_map/terms/pallas_call | solution.py:69
  70.6 5.1 %collective-permute-done.2.refs_0_.refs_5_ = f32[64,1536]{1,0:T(8,128)} collective-permute-done((f32[64,1536]{1,0:T(8,128)}, f32[64,1536]{1,0:T(8,128)}, u32[]{:S(2)}, u32[]{:S(2)}) %collective-permute-start.2) | collective-permute-done | bytes 393248 | tf_op jit(solution)/shard_map/ppermute | solution.py:244
  75.6 1.9 %collective-permute-start.3 = (f32[64,1536]{1,0:T(8,128)}, f32[64,1536]{1,0:T(8,128)}, u32[]{:S(2)}, u32[]{:S(2)}) collective-permute-start(f32[64,1536]{1,0:T(8,128)} %collective-permute-done.2.refs_0_.refs_5_), channel_id=1, source_target_pairs={{0,4},{1,5},{2,6},{3,7},{4,8},{5,9},{6,10},{7,11},{8,12},{9,13},{1... | collective-permute-start | bytes 1179656 | tf_op jit(solution)/shard_map/ppermute | solution.py:248
  77.6 1.9 %terms.7 = (f32[128,256]{1,0:T(8,128)S(1)}, f32[128,16]{1,0:T(8,128)S(1)}) custom-call(f32[64,1536]{1,0:T(8,128)} %collective-permute-done.2.refs_0_.refs_5_, f32[64,1536]{1,0:T(8,128)} %collective-permute-done.6.refs_1_.refs_6_, f32[1536,256]{1,0:T(8,128)S(1)} %copy-done, f32[16,1536]{1,0:T(8,128)S(1)} %bitcast.13), custom_call_target="tpu_custom_call" | custom-call | flops 199999995904 | tf_op jit(solution)/shard_map/terms/pallas_call | solution.py:69
  79.5 7.4 %collective-permute-done.3.refs_0_.refs_7_ = f32[64,1536]{1,0:T(8,128)} collective-permute-done((f32[64,1536]{1,0:T(8,128)}, f32[64,1536]{1,0:T(8,128)}, u32[]{:S(2)}, u32[]{:S(2)}) %collective-permute-start.3) | collective-permute-done | bytes 393248 | tf_op jit(solution)/shard_map/ppermute | solution.py:248
  86.8 4.4 %head_terms.1 = f32[16,40,256]{2,1,0:T(8,128)} custom-call(s32[2]{0:T(128)S(1)} %pad_add_fusion.z_ref, f32[64,1536]{1,0:T(8,128)} %collective-permute-done.3.refs_0_.refs_7_, f32[1536,256]{1,0:T(8,128)S(1)} %copy-done, f32[16,1536]{1,0:T(8,128)S(1)} %bitcast.14, f32[512,768]{1,0:T(8,128)} %bitcast.4.refs_3_.packed_ref, ...), custom_call_target="tpu_custom_call" | custom-call | flops 1000000000 | tf_op jit(solution)/shard_map/head_terms/pallas_call | solution.py:129
  91.3 5.9 %all-to-all-start.3 = ((f32[16,40,256]{2,1,0:T(8,128)}), f32[16,40,256]{2,1,0:T(8,128)S(1)}, u32[]{:S(2)}, u32[]{:S(2)}) async-start(f32[16,40,256]{2,1,0:T(8,128)} %head_terms.1), calls=%async_computation.3 | async-start | bytes 1310720 | tf_op jit(solution)/shard_map/all_to_all | solution.py:253
  97.2 0.0 copy-start.1
  97.2 2.1 %weights.1.refs_8_ = f32[512,256]{1,0:T(8,128)S(1)} custom-call(f32[512,768]{1,0:T(8,128)} %bitcast.4.refs_3_.packed_ref), custom_call_target="tpu_custom_call" | custom-call | flops 1000000000 | tf_op jit(solution)/shard_map/weights/pallas_call | solution.py:88
  99.3 6.0 %below_update.1 = f32[1536,256]{1,0:T(8,128)} custom-call(s32[2]{0:T(128)S(1)} %pad_add_fusion.z_ref, f32[64,1536]{1,0:T(8,128)} %slice.9.refs_0_, f32[64,1536]{1,0:T(8,128)} %collective-permute-done.refs_0_.refs_1_, f32[64,1536]{1,0:T(8,128)} %collective-permute-done.4.refs_1_.refs_2_, f32[64,1536]{1,0:T(8,128)} %collective-permute-done.1.refs_0_.refs_3_, ...), custom_call_target="tpu_custom_call" | custom-call | flops 1207959552 | tf_op jit(solution)/shard_map/below_update/pallas_call | solution.py:153
  105.4 4.1 %all-to-all-done.3.parts_ref = f32[16,40,256]{2,1,0:T(8,128)S(1)} async-done(((f32[16,40,256]{2,1,0:T(8,128)}), f32[16,40,256]{2,1,0:T(8,128)S(1)}, u32[]{:S(2)}, u32[]{:S(2)}) %all-to-all-start.3) | async-done | bytes 655392 | tf_op jit(solution)/shard_map/all_to_all | solution.py:253
  109.5 0.8 finish.1
  (17 shorter events, 0.0 us)
Async XLA Ops:
  1.5 40.1 %copy-start = (f32[1536,256]{1,0:T(8,128)S(1)}, f32[1536,256]{1,0:T(8,128)}, u32[]{:S(2)}) copy-start(f32[1536,256]{1,0:T(8,128)} %refs_1_.2) | copy-start | bytes 4718596
  1.6 40.1 %copy-start.2 = (f32[1536,16]{0,1:T(8,128)S(1)}, f32[1536,16]{0,1:T(8,128)}, u32[]{:S(2)}) copy-start(f32[1536,16]{0,1:T(8,128)} %param.9) | copy-start | bytes 294916
  2.4 20.2 %all-to-all-start = ((f32[4,16,1664]{2,1,0:T(8,128)}), f32[4,16,1664]{2,1,0:T(8,128)S(1)}, u32[]{:S(2)}, u32[]{:S(2)}) async-start(f32[4,16,1664]{2,1,0:T(8,128)} %broadcast_in_dim.4), calls=%async_computation | async-start | bytes 851968 | tf_op jit(solution)/shard_map/all_to_all | solution.py:34
  23.4 20.0 %collective-permute-start = (f32[64,1536]{1,0:T(8,128)}, f32[64,1536]{1,0:T(8,128)}, u32[]{:S(2)}, u32[]{:S(2)}) collective-permute-start(f32[64,1536]{1,0:T(8,128)} %slice.9.refs_0_), channel_id=1, source_target_pairs={{0,4},{1,5},{2,6},{3,7},{4,8},{5,9},{6,10},{7,11},{8,12},{9,13},{1... | collective-permute-start | bytes 1179656 | tf_op jit(solution)/shard_map/ppermute | solution.py:244
  27.9 19.5 %collective-permute-start.4 = (f32[64,1536]{1,0:T(8,128)}, f32[64,1536]{1,0:T(8,128)}, u32[]{:S(2)}, u32[]{:S(2)}) collective-permute-start(f32[64,1536]{1,0:T(8,128)} %slice.9.refs_0_), channel_id=1, source_target_pairs={{0,28},{1,29},{2,30},{3,31},{4,0},{5,1},{6,2},{7,3},{8,4},{9,5},{1... | collective-permute-start | bytes 1179656 | tf_op jit(solution)/shard_map/ppermute | solution.py:245
  37.2 15.8 %all-to-all-start.1 = ((f32[8,64,128]{2,1,0:T(8,128)}), f32[8,64,128]{2,1,0:T(8,128)}, u32[]{:S(2)}, u32[]{:S(2)}) async-start(f32[8,64,128]{2,1,0:T(8,128)} %broadcast_in_dim.5), calls=%async_computation.1 | async-start | bytes 524288 | tf_op jit(solution)/shard_map/all_to_all | solution.py:34
  41.7 11.3 %copy-start.3 = (f32[32,256]{1,0:T(8,128)S(1)}, f32[32,256]{1,0:T(8,128)}, u32[]{:S(2)}) copy-start(f32[32,256]{1,0:T(8,128)} %head_ref.2) | copy-start | bytes 98308
  43.4 18.2 %collective-permute-start.1 = (f32[64,1536]{1,0:T(8,128)}, f32[64,1536]{1,0:T(8,128)}, u32[]{:S(2)}, u32[]{:S(2)}) collective-permute-start(f32[64,1536]{1,0:T(8,128)} %collective-permute-done.refs_0_.refs_1_), channel_id=1, source_target_pairs={{0,4},{1,5},{2,6},{3,7},{4,8},{5,9},{6,10},{7,11},{8,12},{9,13},{1... | collective-permute-start | bytes 1179656 | tf_op jit(solution)/shard_map/ppermute | solution.py:244
  47.3 17.3 %collective-permute-start.5 = (f32[64,1536]{1,0:T(8,128)}, f32[64,1536]{1,0:T(8,128)}, u32[]{:S(2)}, u32[]{:S(2)}) collective-permute-start(f32[64,1536]{1,0:T(8,128)} %collective-permute-done.4.refs_1_.refs_2_), channel_id=1, source_target_pairs={{0,28},{1,29},{2,30},{3,31},{4,0},{5,1},{6,2},{7,3},{8,4},{9,5},{1... | collective-permute-start | bytes 1179656 | tf_op jit(solution)/shard_map/ppermute | solution.py:245
  55.2 31.6 %all-to-all-start.2 = ((f32[16,32,768]{2,1,0:T(8,128)}), f32[16,32,768]{2,1,0:T(8,128)}, u32[]{:S(2)}, u32[]{:S(2)}) async-start(f32[16,32,768]{2,1,0:T(8,128)} %packed_copies.1), calls=%async_computation.2 | async-start | bytes 3145728 | tf_op jit(solution)/shard_map/all_to_all | solution.py:34
  61.6 14.0 %collective-permute-start.2 = (f32[64,1536]{1,0:T(8,128)}, f32[64,1536]{1,0:T(8,128)}, u32[]{:S(2)}, u32[]{:S(2)}) collective-permute-start(f32[64,1536]{1,0:T(8,128)} %collective-permute-done.1.refs_0_.refs_3_), channel_id=1, source_target_pairs={{0,4},{1,5},{2,6},{3,7},{4,8},{5,9},{6,10},{7,11},{8,12},{9,13},{1... | collective-permute-start | bytes 1179656 | tf_op jit(solution)/shard_map/ppermute | solution.py:244
  64.6 13.0 %collective-permute-start.6 = (f32[64,1536]{1,0:T(8,128)}, f32[64,1536]{1,0:T(8,128)}, u32[]{:S(2)}, u32[]{:S(2)}) collective-permute-start(f32[64,1536]{1,0:T(8,128)} %collective-permute-done.5.refs_1_.refs_4_), channel_id=1, source_target_pairs={{0,28},{1,29},{2,30},{3,31},{4,0},{5,1},{6,2},{7,3},{8,4},{9,5},{1... | collective-permute-start | bytes 1179656 | tf_op jit(solution)/shard_map/ppermute | solution.py:245
  75.6 11.2 %collective-permute-start.3 = (f32[64,1536]{1,0:T(8,128)}, f32[64,1536]{1,0:T(8,128)}, u32[]{:S(2)}, u32[]{:S(2)}) collective-permute-start(f32[64,1536]{1,0:T(8,128)} %collective-permute-done.2.refs_0_.refs_5_), channel_id=1, source_target_pairs={{0,4},{1,5},{2,6},{3,7},{4,8},{5,9},{6,10},{7,11},{8,12},{9,13},{1... | collective-permute-start | bytes 1179656 | tf_op jit(solution)/shard_map/ppermute | solution.py:248
  91.3 18.2 %all-to-all-start.3 = ((f32[16,40,256]{2,1,0:T(8,128)}), f32[16,40,256]{2,1,0:T(8,128)S(1)}, u32[]{:S(2)}, u32[]{:S(2)}) async-start(f32[16,40,256]{2,1,0:T(8,128)} %head_terms.1), calls=%async_computation.3 | async-start | bytes 1310720 | tf_op jit(solution)/shard_map/all_to_all | solution.py:253
  97.2 2.1 %copy-start.1 = (f32[1536,256]{1,0:T(8,128)S(1)}, f32[1536,256]{1,0:T(8,128)}, u32[]{:S(2)}) copy-start(f32[1536,256]{1,0:T(8,128)} %refs_9_.1) | copy-start | bytes 4718596
  99.3 10.2 %copy-start.4 = (f32[32,256]{1,0:T(8,128)S(1)}, f32[32,256]{1,0:T(8,128)}, u32[]{:S(2)}) copy-start(f32[32,256]{1,0:T(8,128)} %head_ref.3) | copy-start | bytes 98308
  99.3 10.2 %copy-start.5 = (f32[32,16]{0,1:T(8,128)S(1)}, f32[32,16]{0,1:T(8,128)}, u32[]{:S(2)}) copy-start(f32[32,16]{0,1:T(8,128)} %param.13) | copy-start | bytes 6148

commit v4 on v3

--- a/solution.py
+++ b/solution.py
@@ -78,15 +78,15 @@
     )(*pieces, b, f)
 
 
-def weight_kernel(width, packed_ref, w_ref):
-    inverse = split(packed_ref[:, width:])
-    w_ref[...] = dot3(inverse, split(packed_ref[:, :width]), ((1,), (0,)))
+def weight_kernel(packed_ref, w_ref):
+    nb = packed_ref.shape[0]
+    w_ref[...] = dot3(split(packed_ref[:, :nb]), split(packed_ref[:, nb:]), ((1,), (0,)))
 
 
 def weights(packed, width):
     nb = packed.shape[0]
     return pl.pallas_call(
-        functools.partial(weight_kernel, width),
+        weight_kernel,
         out_shape=jax.ShapeDtypeStruct((nb, width), jnp.float32),
         compiler_params=params(),
         cost_estimate=pl.CostEstimate(flops=10**9, bytes_accessed=0, transcendentals=0),
@@ -100,10 +100,10 @@
 
 
 def head_kernel(group, z_ref, *refs):
-    piece_ref, b_ref, f_ref, packed_ref = refs[:4]
+    piece_ref, b_ref, f_ref, inverse_ref = refs[:4]
     found = refs[4:12]
     out_ref, t_scr, s_scr = refs[12:]
-    turned = split(packed_ref[:, b_ref.shape[1] :].T)
+    turned = split(inverse_ref[...].T)
     for step in range(ZS // 2):
         t_ref, s_ref = found[2 * step], found[2 * step + 1]
         for part, offset in enumerate((0,) if step == 0 else (step, -step)):
@@ -130,8 +130,11 @@
         functools.partial(head_kernel, nb // ZS),
         out_shape=jax.ShapeDtypeStruct((RS, nb // RS + 8, width), jnp.float32),
         in_specs=[pl.BlockSpec(memory_space=pltpu.SMEM)]
-        + [pl.BlockSpec(memory_space=pltpu.VMEM)] * len(args),
+        + [pl.BlockSpec(memory_space=pltpu.VMEM)] * 3
+        + [pl.BlockSpec((nb, nb), lambda i: (0, 0))]
+        + [pl.BlockSpec(memory_space=pltpu.VMEM)] * len(found),
         out_specs=pl.BlockSpec(memory_space=pltpu.VMEM),
+        grid=(1,),
         scratch_shapes=[pltpu.VMEM((nb, width), jnp.float32), pltpu.VMEM((nb, small), jnp.float32)],
         compiler_params=params(),
         cost_estimate=pl.CostEstimate(flops=10**9, bytes_accessed=0, transcendentals=0),
@@ -192,11 +195,11 @@
 
 
 def packed_kernel(head_ref, inverse_ref, out_ref):
-    rows, width = head_ref.shape
-    inverse = inverse_ref[...].T[:rows]
-    for k in range(RS):
-        out_ref[k, :, :width] = head_ref[...]
-        out_ref[k, :, width:] = inverse
+    inverse = inverse_ref[...].T[: head_ref.shape[0]]
+    nb = inverse.shape[1]
+    for k in range(out_ref.shape[0]):
+        out_ref[k, :, :nb] = inverse
+        out_ref[k, :, nb:] = head_ref[...]
 
 
 def packed_copies(head, inverse):
@@ -204,7 +207,13 @@
     nb = inverse.shape[0]
     return pl.pallas_call(
         packed_kernel,
-        out_shape=jax.ShapeDtypeStruct((RS, rows, width + nb), jnp.float32),
+        grid=(4,),
+        out_shape=jax.ShapeDtypeStruct((RS, rows, nb + width), jnp.float32),
+        in_specs=[
+            pl.BlockSpec(head.shape, lambda i: (0, 0)),
+            pl.BlockSpec(inverse.shape, lambda i: (0, 0)),
+        ],
+        out_specs=pl.BlockSpec((RS // 4, rows, nb + width), lambda i: (i, 0, 0)),
         compiler_params=params(),
         cost_estimate=pl.CostEstimate(flops=10**8, bytes_accessed=0, transcendentals=0),
         name="packed_copies",
@@ -237,16 +246,25 @@
     inverse = exchange(inverse, "col", far).reshape(nb, 128)
     copies, later_factor = lax.optimization_barrier((packed_copies(head_factor, inverse), below_factor))
     packed = exchange(copies, "row", None).reshape(nb, width + nb)
-    one = other = part[:, :length]
-    pieces = [one]
-    found = terms((one,), below_factor, factor, COSTS[0])
+    found = {}
+    ring = [part[:, :length]] * 2
+    pieces = ring[:1]
+    held = [ring[:1]]
     for step in range(1, ZS // 2):
-        one = lax.ppermute(one, ("row", "col"), along_z(1))
-        other = lax.ppermute(other, ("row", "col"), along_z(-1))
-        found += tuple(terms((one, other), later_factor, factor, COSTS[step]))
-        pieces += [one, other]
-    one = lax.ppermute(one, ("row", "col"), along_z(1))
+        ring = [lax.ppermute(x, ("row", "col"), along_z(way)) for x, way in zip(ring, (1, -1))]
+        if step > 1:
+            ring[0], later_factor = lax.optimization_barrier((ring[0], later_factor))
+        held.append(ring)
+        pieces += ring
+        if step == 2:
+            found[1] = terms(held[1], later_factor, factor, COSTS[1])
+            found[2] = terms(held[2], later_factor, factor, COSTS[2])
+        if step == 3:
+            found[0] = terms(held[0], later_factor, factor, COSTS[0])
+            found[3] = terms(held[3], later_factor, factor, COSTS[3])
+    one = lax.ppermute(ring[0], ("row", "col"), along_z(1))
     pieces.append(one)
+    found = [x for step in range(ZS // 2) for x in found[step]]
     local = head_terms(z, one, later_factor, factor, packed, tuple(found))
     packed, local = lax.optimization_barrier((packed, local))
     weight = weights(packed, width)

time: 111 us -> 111 us (level)
  the two profiles are of different devices: /device:TPU:16 before, /device:TPU:1 now
where the time goes in v4:
time: 111 us; the launch traced here: 110 us
  starting transfers between devices  53 us (48%)
  Pallas kernels  20.1 us (18%)
  blocking collectives  19.5 us (18%)
  waiting for transfers between devices  14.5 us (13%)
    ppermute x6, starting transfers between devices, on_device(): lax.ppermute(x, ('row', 'col'), along_z(way))  25.2 us
    all_to_all x1, blocking collectives, exchange(): lax.all_to_all(copies, axis, 0, 0, tiled=True, axis_index_groups=groups)  19.5 us
    all_to_all x2, starting transfers between devices, exchange(): lax.all_to_all(copies, axis, 0, 0, tiled=True, axis_index_groups=groups)  15.9 us
    all_to_all x1, starting transfers between devices, on_device(): parts = lax.all_to_all(local, 'row', 0, 0, tiled=True)  10 us
    pallas_call x1, Pallas kernels, below_update(): pl.pallas_call(functools.partial(below_kernel, nb // ZS), grid=(length //...  5.9 us
    ppermute x6, waiting for transfers between devices, on_device(): lax.ppermute(x, ('row', 'col'), along_z(way))  5.61 us
    pallas_call x4, Pallas kernels, terms(): pl.pallas_call(functools.partial(term_kernel, len(pieces)), out_shape=(ja...  5.22 us
    pallas_call x1, Pallas kernels, head_terms(): pl.pallas_call(functools.partial(head_kernel, nb // ZS), out_shape=jax.Sh...  4.24 us
  transfers between devices with their start and end apart: 10, of which 7 were waited for; matrix products, arithmetic and copies ran while one was open for 1% of the time, Pallas kernels for 14%

profile of v4, /device:TPU:1, one launch (start us, length us, event | category | flops | bytes accessed | tf_op | source)
XLA Modules:
  0.0 109.8 jit_solution(6163528518239201962)
XLA Ops:
  0.6 0.9 select_maximum_fusion
  1.6 19.5 %all_to_all.20 = f32[4,16,1664]{2,1,0:T(8,128)S(1)} all-to-all(f32[4,16,1664]{2,1,0:T(8,128)S(1)} %broadcast_in_dim.4), channel_id=1, replica_groups={{0,1,2,3},{4,5,6,7},{8,9,10,11},{12,13,14,15},{16,17,18,19},{20,21,22,2..., dimensions={0} | all-to-all | bytes 851968 | tf_op jit(solution)/shard_map/all_to_all | solution.py:34
  21.1 11.5 %collective-permute-start = (f32[64,1536]{1,0:T(8,128)S(1)}, f32[64,1536]{1,0:T(8,128)S(1)}, u32[]{:S(2)}, u32[]{:S(2)}) collective-permute-start(f32[64,1536]{1,0:T(8,128)S(1)} %slice.9.refs_0_), channel_id=1, source_target_pairs={{0,4},{1,5},{2,6},{3,7},{4,8},{5,9},{6,10},{7,11},{8,12},{9,13},{1... | collective-permute-start | bytes 1179656 | tf_op jit(solution)/shard_map/ppermute | solution.py:254
  32.6 1.9 %collective-permute-start.4 = (f32[64,1536]{1,0:T(8,128)S(1)}, f32[64,1536]{1,0:T(8,128)S(1)}, u32[]{:S(2)}, u32[]{:S(2)}) collective-permute-start(f32[64,1536]{1,0:T(8,128)S(1)} %slice.9.refs_0_), channel_id=1, source_target_pairs={{0,28},{1,29},{2,30},{3,31},{4,0},{5,1},{6,2},{7,3},{8,4},{9,5},{1... | collective-permute-start | bytes 1179656 | tf_op jit(solution)/shard_map/ppermute | solution.py:254
  34.6 0.7 broadcast_in_dim.5
  35.3 3.9 %all-to-all-start.1 = ((f32[8,64,128]{2,1,0:T(8,128)}), f32[8,64,128]{2,1,0:T(8,128)S(1)}, u32[]{:S(2)}, u32[]{:S(2)}) async-start(f32[8,64,128]{2,1,0:T(8,128)} %broadcast_in_dim.5), calls=%async_computation.1 | async-start | bytes 524288 | tf_op jit(solution)/shard_map/all_to_all | solution.py:34
  39.2 4.6 %collective-permute-start.1 = (f32[64,1536]{1,0:T(8,128)S(1)}, f32[64,1536]{1,0:T(8,128)}, u32[]{:S(2)}, u32[]{:S(2)}) collective-permute-start(f32[64,1536]{1,0:T(8,128)S(1)} %collective-permute-done.refs_0_.refs_1_), channel_id=1, source_target_pairs={{0,4},{1,5},{2,6},{3,7},{4,8},{5,9},{6,10},{7,11},{8,12},{9,13},{1... | collective-permute-start | bytes 1179656 | tf_op jit(solution)/shard_map/ppermute | solution.py:254
  43.8 1.1 collective-permute-done.4.refs_1_.refs_2_
  44.9 1.9 %collective-permute-start.5 = (f32[64,1536]{1,0:T(8,128)S(1)}, f32[64,1536]{1,0:T(8,128)}, u32[]{:S(2)}, u32[]{:S(2)}) collective-permute-start(f32[64,1536]{1,0:T(8,128)S(1)} %collective-permute-done.4.refs_1_.refs_2_), channel_id=1, source_target_pairs={{0,28},{1,29},{2,30},{3,31},{4,0},{5,1},{6,2},{7,3},{8,4},{9,5},{1... | collective-permute-start | bytes 1179656 | tf_op jit(solution)/shard_map/ppermute | solution.py:254
  46.8 0.1 pad_add_fusion.z_ref
  46.9 0.9 all-to-all-done.1
  47.8 1.8 %packed_copies.1 = f32[16,32,768]{2,1,0:T(8,128)} custom-call(f32[32,256]{1,0:T(8,128)S(1)} %copy-done.6, f32[512,128]{1,0:T(8,128)S(1)} %bitcast.10), custom_call_target="tpu_custom_call" | custom-call | flops 100000000 | tf_op jit(solution)/shard_map/packed_copies/pallas_call | solution.py:208
  49.7 12.0 %all-to-all-start.2 = ((f32[16,32,768]{2,1,0:T(8,128)}), f32[16,32,768]{2,1,0:T(8,128)}, u32[]{:S(2)}, u32[]{:S(2)}) async-start(f32[16,32,768]{2,1,0:T(8,128)} %packed_copies.1), calls=%async_computation.2 | async-start | bytes 3145728 | tf_op jit(solution)/shard_map/all_to_all | solution.py:34
  61.6 1.9 %collective-permute-start.2 = (f32[64,1536]{1,0:T(8,128)}, f32[64,1536]{1,0:T(8,128)}, u32[]{:S(2)}, u32[]{:S(2)}) collective-permute-start(f32[64,1536]{1,0:T(8,128)} %collective-permute-done.1.refs_0_.refs_3_), channel_id=1, source_target_pairs={{0,4},{1,5},{2,6},{3,7},{4,8},{5,9},{6,10},{7,11},{8,12},{9,13},{1... | collective-permute-start | bytes 1179656 | tf_op jit(solution)/shard_map/ppermute | solution.py:254
  63.6 3.4 %collective-permute-start.6 = (f32[64,1536]{1,0:T(8,128)}, f32[64,1536]{1,0:T(8,128)}, u32[]{:S(2)}, u32[]{:S(2)}) collective-permute-start(f32[64,1536]{1,0:T(8,128)} %collective-permute-done.5.refs_1_.refs_4_), channel_id=1, source_target_pairs={{0,28},{1,29},{2,30},{3,31},{4,0},{5,1},{6,2},{7,3},{8,4},{9,5},{1... | collective-permute-start | bytes 1179656 | tf_op jit(solution)/shard_map/ppermute | solution.py:254
  66.9 1.9 %terms.6 = (f32[128,256]{1,0:T(8,128)S(1)}, f32[128,16]{1,0:T(8,128)S(1)}) custom-call(f32[64,1536]{1,0:T(8,128)} %collective-permute-done.1.refs_0_.refs_3_, f32[64,1536]{1,0:T(8,128)} %collective-permute-done.5.refs_1_.refs_4_, f32[1536,256]{1,0:T(8,128)S(1)} %copy-done, f32[16,1536]{1,0:T(8,128)S(1)} %bitcast.11), custom_call_target="tpu_custom_call" | custom-call | flops 199999995904 | tf_op jit(solution)/shard_map/terms/pallas_call | solution.py:69
  68.8 0.8 terms.5
  69.6 2.7 %collective-permute-done.2.refs_0_.refs_5_ = f32[64,1536]{1,0:T(8,128)} collective-permute-done((f32[64,1536]{1,0:T(8,128)}, f32[64,1536]{1,0:T(8,128)}, u32[]{:S(2)}, u32[]{:S(2)}) %collective-permute-start.2) | collective-permute-done | bytes 393248 | tf_op jit(solution)/shard_map/ppermute | solution.py:254
  72.3 0.7 terms.4
  73.1 1.9 %collective-permute-start.3 = (f32[64,1536]{1,0:T(8,128)}, f32[64,1536]{1,0:T(8,128)}, u32[]{:S(2)}, u32[]{:S(2)}) collective-permute-start(f32[64,1536]{1,0:T(8,128)} %collective-permute-done.2.refs_0_.refs_5_), channel_id=1, source_target_pairs={{0,4},{1,5},{2,6},{3,7},{4,8},{5,9},{6,10},{7,11},{8,12},{9,13},{1... | collective-permute-start | bytes 1179656 | tf_op jit(solution)/shard_map/ppermute | solution.py:265
  75.0 1.8 %collective-permute-done.6.refs_1_.refs_6_ = f32[64,1536]{1,0:T(8,128)} collective-permute-done((f32[64,1536]{1,0:T(8,128)}, f32[64,1536]{1,0:T(8,128)}, u32[]{:S(2)}, u32[]{:S(2)}) %collective-permute-start.6) | collective-permute-done | bytes 393248 | tf_op jit(solution)/shard_map/ppermute | solution.py:254
  76.8 1.9 %terms.7 = (f32[128,256]{1,0:T(8,128)S(1)}, f32[128,16]{1,0:T(8,128)S(1)}) custom-call(f32[64,1536]{1,0:T(8,128)} %collective-permute-done.2.refs_0_.refs_5_, f32[64,1536]{1,0:T(8,128)} %collective-permute-done.6.refs_1_.refs_6_, f32[1536,256]{1,0:T(8,128)S(1)} %copy-done, f32[16,1536]{1,0:T(8,128)S(1)} %bitcast.14), custom_call_target="tpu_custom_call" | custom-call | flops 199999995904 | tf_op jit(solution)/shard_map/terms/pallas_call | solution.py:69
  78.7 3.2 %collective-permute-done.3.refs_0_.refs_7_ = f32[64,1536]{1,0:T(8,128)} collective-permute-done((f32[64,1536]{1,0:T(8,128)}, f32[64,1536]{1,0:T(8,128)}, u32[]{:S(2)}, u32[]{:S(2)}) %collective-permute-start.3) | collective-permute-done | bytes 393248 | tf_op jit(solution)/shard_map/ppermute | solution.py:265
  81.9 1.6 %all-to-all-done.2 = f32[16,32,768]{2,1,0:T(8,128)} async-done(((f32[16,32,768]{2,1,0:T(8,128)}), f32[16,32,768]{2,1,0:T(8,128)}, u32[]{:S(2)}, u32[]{:S(2)}) %all-to-all-start.2) | async-done | bytes 1572896 | tf_op jit(solution)/shard_map/all_to_all | solution.py:34
  83.5 4.2 %head_terms.1 = f32[16,40,256]{2,1,0:T(8,128)} custom-call(s32[2]{0:T(128)S(1)} %pad_add_fusion.z_ref, f32[64,1536]{1,0:T(8,128)} %collective-permute-done.3.refs_0_.refs_7_, f32[1536,256]{1,0:T(8,128)S(1)} %copy-done, f32[16,1536]{1,0:T(8,128)S(1)} %bitcast.15, f32[512,768]{1,0:T(8,128)} %bitcast.4.refs_3_.packed_ref, ...), custom_call_target="tpu_custom_call" | custom-call | flops 1000000000 | tf_op jit(solution)/shard_map/head_terms/pallas_call | solution.py:129
  87.8 10.0 %all-to-all-start.3 = ((f32[16,40,256]{2,1,0:T(8,128)}), f32[16,40,256]{2,1,0:T(8,128)S(1)}, u32[]{:S(2)}, u32[]{:S(2)}) async-start(f32[16,40,256]{2,1,0:T(8,128)} %head_terms.1), calls=%async_computation.3 | async-start | bytes 1310720 | tf_op jit(solution)/shard_map/all_to_all | solution.py:271
  97.8 2.1 %weights.1.refs_8_ = f32[512,256]{1,0:T(8,128)S(1)} custom-call(f32[512,768]{1,0:T(8,128)} %bitcast.4.refs_3_.packed_ref), custom_call_target="tpu_custom_call" | custom-call | flops 1000000000 | tf_op jit(solution)/shard_map/weights/pallas_call | solution.py:88
  99.9 0.0 copy-start.7
  99.9 0.0 copy-start.8
  100.0 5.9 %below_update.1 = f32[1536,256]{1,0:T(8,128)} custom-call(s32[2]{0:T(128)S(1)} %pad_add_fusion.z_ref, f32[64,1536]{1,0:T(8,128)S(1)} %copy-done.4, f32[64,1536]{1,0:T(8,128)S(1)} %collective-permute-done.refs_0_.refs_1_, f32[64,1536]{1,0:T(8,128)S(1)} %collective-permute-done.4.refs_1_.refs_2_, f32[64,1536]{1,0:T(8,128)} %collective-permute-done.1.refs_0_.refs_3_, ...), custom_call_target="tpu_custom_call" | custom-call | flops 1207959552 | tf_op jit(solution)/shard_map/below_update/pallas_call | solution.py:156
  105.8 3.1 %all-to-all-done.3.parts_ref = f32[16,40,256]{2,1,0:T(8,128)S(1)} async-done(((f32[16,40,256]{2,1,0:T(8,128)}), f32[16,40,256]{2,1,0:T(8,128)S(1)}, u32[]{:S(2)}, u32[]{:S(2)}) %all-to-all-start.3) | async-done | bytes 655392 | tf_op jit(solution)/shard_map/all_to_all | solution.py:271
  109.0 0.8 finish.1
  (22 shorter events, 0.1 us)
Async XLA Ops:
  1.5 46.3 %copy-start.6 = (f32[32,256]{1,0:T(8,128)S(1)}, f32[32,256]{1,0:T(8,128)}, u32[]{:S(2)}) copy-start(f32[32,256]{1,0:T(8,128)} %head_ref.2) | copy-start | bytes 98308
  21.1 26.7 %copy-start.2 = (f32[64,1536]{1,0:T(8,128)}, f32[64,1536]{1,0:T(8,128)S(1)}, u32[]{:S(2)}) copy-start(f32[64,1536]{1,0:T(8,128)S(1)} %slice.9.refs_0_) | copy-start | bytes 1179652
  21.1 18.1 %collective-permute-start = (f32[64,1536]{1,0:T(8,128)S(1)}, f32[64,1536]{1,0:T(8,128)S(1)}, u32[]{:S(2)}, u32[]{:S(2)}) collective-permute-start(f32[64,1536]{1,0:T(8,128)S(1)} %slice.9.refs_0_), channel_id=1, source_target_pairs={{0,4},{1,5},{2,6},{3,7},{4,8},{5,9},{6,10},{7,11},{8,12},{9,13},{1... | collective-permute-start | bytes 1179656 | tf_op jit(solution)/shard_map/ppermute | solution.py:254
  32.6 12.3 %collective-permute-start.4 = (f32[64,1536]{1,0:T(8,128)S(1)}, f32[64,1536]{1,0:T(8,128)S(1)}, u32[]{:S(2)}, u32[]{:S(2)}) collective-permute-start(f32[64,1536]{1,0:T(8,128)S(1)} %slice.9.refs_0_), channel_id=1, source_target_pairs={{0,28},{1,29},{2,30},{3,31},{4,0},{5,1},{6,2},{7,3},{8,4},{9,5},{1... | collective-permute-start | bytes 1179656 | tf_op jit(solution)/shard_map/ppermute | solution.py:254
  35.3 12.5 %all-to-all-start.1 = ((f32[8,64,128]{2,1,0:T(8,128)}), f32[8,64,128]{2,1,0:T(8,128)S(1)}, u32[]{:S(2)}, u32[]{:S(2)}) async-start(f32[8,64,128]{2,1,0:T(8,128)} %broadcast_in_dim.5), calls=%async_computation.1 | async-start | bytes 524288 | tf_op jit(solution)/shard_map/all_to_all | solution.py:34
  39.2 22.4 %collective-permute-start.1 = (f32[64,1536]{1,0:T(8,128)S(1)}, f32[64,1536]{1,0:T(8,128)}, u32[]{:S(2)}, u32[]{:S(2)}) collective-permute-start(f32[64,1536]{1,0:T(8,128)S(1)} %collective-permute-done.refs_0_.refs_1_), channel_id=1, source_target_pairs={{0,4},{1,5},{2,6},{3,7},{4,8},{5,9},{6,10},{7,11},{8,12},{9,13},{1... | collective-permute-start | bytes 1179656 | tf_op jit(solution)/shard_map/ppermute | solution.py:254
  44.9 18.7 %collective-permute-start.5 = (f32[64,1536]{1,0:T(8,128)S(1)}, f32[64,1536]{1,0:T(8,128)}, u32[]{:S(2)}, u32[]{:S(2)}) collective-permute-start(f32[64,1536]{1,0:T(8,128)S(1)} %collective-permute-done.4.refs_1_.refs_2_), channel_id=1, source_target_pairs={{0,28},{1,29},{2,30},{3,31},{4,0},{5,1},{6,2},{7,3},{8,4},{9,5},{1... | collective-permute-start | bytes 1179656 | tf_op jit(solution)/shard_map/ppermute | solution.py:254
  49.7 17.3 %copy-start = (f32[1536,256]{1,0:T(8,128)S(1)}, f32[1536,256]{1,0:T(8,128)}, u32[]{:S(2)}) copy-start(f32[1536,256]{1,0:T(8,128)} %refs_1_.1) | copy-start | bytes 4718596
  49.7 17.3 %copy-start.5 = (f32[1536,16]{0,1:T(8,128)S(1)}, f32[1536,16]{0,1:T(8,128)}, u32[]{:S(2)}) copy-start(f32[1536,16]{0,1:T(8,128)} %param.9) | copy-start | bytes 294916
  49.7 33.9 %all-to-all-start.2 = ((f32[16,32,768]{2,1,0:T(8,128)}), f32[16,32,768]{2,1,0:T(8,128)}, u32[]{:S(2)}, u32[]{:S(2)}) async-start(f32[16,32,768]{2,1,0:T(8,128)} %packed_copies.1), calls=%async_computation.2 | async-start | bytes 3145728 | tf_op jit(solution)/shard_map/all_to_all | solution.py:34
  61.6 10.7 %collective-permute-start.2 = (f32[64,1536]{1,0:T(8,128)}, f32[64,1536]{1,0:T(8,128)}, u32[]{:S(2)}, u32[]{:S(2)}) collective-permute-start(f32[64,1536]{1,0:T(8,128)} %collective-permute-done.1.refs_0_.refs_3_), channel_id=1, source_target_pairs={{0,4},{1,5},{2,6},{3,7},{4,8},{5,9},{6,10},{7,11},{8,12},{9,13},{1... | collective-permute-start | bytes 1179656 | tf_op jit(solution)/shard_map/ppermute | solution.py:254
  63.6 13.2 %collective-permute-start.6 = (f32[64,1536]{1,0:T(8,128)}, f32[64,1536]{1,0:T(8,128)}, u32[]{:S(2)}, u32[]{:S(2)}) collective-permute-start(f32[64,1536]{1,0:T(8,128)} %collective-permute-done.5.refs_1_.refs_4_), channel_id=1, source_target_pairs={{0,28},{1,29},{2,30},{3,31},{4,0},{5,1},{6,2},{7,3},{8,4},{9,5},{1... | collective-permute-start | bytes 1179656 | tf_op jit(solution)/shard_map/ppermute | solution.py:254
  68.8 3.5 %copy-start.3 = (f32[64,1536]{1,0:T(8,128)S(1)}, f32[64,1536]{1,0:T(8,128)}, u32[]{:S(2)}) copy-start(f32[64,1536]{1,0:T(8,128)} %copy-done.2) | copy-start | bytes 1179652
  73.1 8.8 %collective-permute-start.3 = (f32[64,1536]{1,0:T(8,128)}, f32[64,1536]{1,0:T(8,128)}, u32[]{:S(2)}, u32[]{:S(2)}) collective-permute-start(f32[64,1536]{1,0:T(8,128)} %collective-permute-done.2.refs_0_.refs_5_), channel_id=1, source_target_pairs={{0,4},{1,5},{2,6},{3,7},{4,8},{5,9},{6,10},{7,11},{8,12},{9,13},{1... | collective-permute-start | bytes 1179656 | tf_op jit(solution)/shard_map/ppermute | solution.py:265
  87.8 21.2 %all-to-all-start.3 = ((f32[16,40,256]{2,1,0:T(8,128)}), f32[16,40,256]{2,1,0:T(8,128)S(1)}, u32[]{:S(2)}, u32[]{:S(2)}) async-start(f32[16,40,256]{2,1,0:T(8,128)} %head_terms.1), calls=%async_computation.3 | async-start | bytes 1310720 | tf_op jit(solution)/shard_map/all_to_all | solution.py:271
  97.8 2.2 %copy-start.1 = (f32[1536,256]{1,0:T(8,128)S(1)}, f32[1536,256]{1,0:T(8,128)}, u32[]{:S(2)}) copy-start(f32[1536,256]{1,0:T(8,128)} %refs_9_.1) | copy-start | bytes 4718596
  97.8 2.2 %copy-start.4 = (f32[64,1536]{1,0:T(8,128)S(1)}, f32[64,1536]{1,0:T(8,128)}, u32[]{:S(2)}) copy-start(f32[64,1536]{1,0:T(8,128)} %copy-done.2) | copy-start | bytes 1179652
  99.9 9.1 %copy-start.7 = (f32[32,256]{1,0:T(8,128)S(1)}, f32[32,256]{1,0:T(8,128)}, u32[]{:S(2)}) copy-start(f32[32,256]{1,0:T(8,128)} %head_ref.3) | copy-start | bytes 98308
  99.9 9.1 %copy-start.8 = (f32[32,16]{0,1:T(8,128)S(1)}, f32[32,16]{0,1:T(8,128)}, u32[]{:S(2)}) copy-start(f32[32,16]{0,1:T(8,128)} %param.13) | copy-start | bytes 6148
